TPU v7x, 768 devices: a whole 4x8x12 slice. The times are simulated.
768 devices in a mesh: lon: 192 (over x, z, y_hi, core), tm: 4 (over y_lo).
Axes of the slice: x: 4, y: 8 (y_hi: 2, y_lo: 4; y = y_hi * 4 + y_lo), z: 12, core: 2. Of those that a mesh axis runs over, the one named last changes fastest.
Arguments:
- right_side: float32 [1536, 96, 256], P('lon', 'tm'), may hold values from -40 to 40
- kappa_squared: float32 [1536, 96, 256], P('lon', 'tm'), may hold values from 0.05 to 0.5
- hdiff: float32 [1536, 96, 256], P('lon', 'tm'), may hold values from 0.1 to 0.4
- obs_weight: float32 [1536, 96, 256], P('lon', 'tm'), may hold values from 0.2 to 2
Outputs:
- solution_field: float32 [1536, 96, 256], P('lon', 'tm')
- residual: float32 [1536, 96, 256], P('lon', 'tm')
All inputs are finite; a program needn't handle non-finite values.
Results may differ from a plain program's by a relative error of at most 0.033.
Values sent between devices are 32-bit elements; how exact they have to be, the bound alone decides.
A program may use at most 32 MiB of HBM per device.

v0:
```python
import jax
import jax.numpy as jnp
from jax import lax
from jax.sharding import PartitionSpec as P

ITERS = 3


def padded(cells, sides, width):
    for axis, dim in sides:
        count = lax.axis_size(axis)
        head = lax.slice_in_dim(cells, 0, width, axis=dim)
        tail = lax.slice_in_dim(cells, cells.shape[dim] - width, cells.shape[dim], axis=dim)
        cells = jnp.concatenate(
            [
                lax.ppermute(tail, axis, [(i, (i + 1) % count) for i in range(count)]),
                cells,
                lax.ppermute(head, axis, [((i + 1) % count, i) for i in range(count)]),
            ],
            axis=dim,
        )
    return cells


def face(here, there):
    total = here + there
    safe = jnp.where(total > 0, total, 1.0)
    return jnp.where(total > 0, 2.0 * here * there / safe, 0.0)


def lat_next(a, step):
    zeros = jnp.zeros_like(a[:, :, :1])
    if step > 0:
        return jnp.concatenate([a[:, :, 1:], zeros], axis=2)
    return jnp.concatenate([zeros, a[:, :, :-1]], axis=2)


def face_set(hpad):
    middle_part = hpad[1:-1, 1:-1]
    return (
        face(middle_part, hpad[2:, 1:-1]),
        face(middle_part, hpad[:-2, 1:-1]),
        face(middle_part, hpad[1:-1, 2:]),
        face(middle_part, hpad[1:-1, :-2]),
        face(middle_part, lat_next(middle_part, 1)),
        face(middle_part, lat_next(middle_part, -1)),
    )


def stencil_apply(vector_padded, kappa_field, face_values):
    middle_part = vector_padded[1:-1, 1:-1]
    remaining_terms = (
        vector_padded[2:, 1:-1],
        vector_padded[:-2, 1:-1],
        vector_padded[1:-1, 2:],
        vector_padded[1:-1, :-2],
        lat_next(middle_part, 1),
        lat_next(middle_part, -1),
    )
    total = kappa_field * middle_part
    for coeff, other in zip(face_values, remaining_terms):
        total = total + coeff * (middle_part - other)
    return total


def seal_time(hpad, width, steps):
    first = lax.axis_index("tm") == 0
    final = lax.axis_index("tm") == lax.axis_size("tm") - 1
    place = jnp.arange(steps + 2 * width)
    outside = first & (place < width) | final & (place >= steps + width)
    return jnp.where(outside[None, :, None], 0.0, hpad)


def body(right_side, kappa_squared, hdiff, obs_weight):
    steps = right_side.shape[1]
    hpad = padded(hdiff, (("lon", 0), ("tm", 1)), 1)
    face_values = face_set(seal_time(hpad, 1, steps))

    def apply_once(vector_input):
        vector_padded = padded(vector_input, (("lon", 0), ("tm", 1)), 1)
        return stencil_apply(vector_padded, kappa_squared, face_values)

    def precision(vector_input):
        return apply_once(apply_once(vector_input)) + obs_weight * vector_input

    diag_l = (
        kappa_squared
        + face_values[0]
        + face_values[1]
        + face_values[2]
        + face_values[3]
        + face_values[4]
        + face_values[5]
    )
    squares = (
        face_values[0] ** 2
        + face_values[1] ** 2
        + face_values[2] ** 2
        + face_values[3] ** 2
        + face_values[4] ** 2
        + face_values[5] ** 2
    )
    inverse = 1.0 / (diag_l * diag_l + squares + obs_weight)

    def two_sums(residual, scaled, image):
        return lax.psum((jnp.sum(residual * scaled), jnp.sum(image * scaled)), ("lon", "tm"))

    residual = right_side
    scaled = inverse * residual
    image = precision(scaled)
    gamma, curvature = two_sums(residual, scaled, image)
    alpha = gamma / curvature
    direction = scaled
    along = image
    solution_field = alpha * direction
    residual = residual - alpha * along
    for step in range(1, ITERS):
        scaled = inverse * residual
        image = precision(scaled)
        gamma_next, curvature = two_sums(residual, scaled, image)
        ratio = gamma_next / gamma
        alpha = gamma_next / (curvature - ratio * gamma_next / alpha)
        direction = scaled + ratio * direction
        along = image + ratio * along
        solution_field = solution_field + alpha * direction
        residual = residual - alpha * along
        gamma = gamma_next
    return (solution_field, residual)


def solution(mesh):
    placed = (
        P("lon", "tm", None),
        P("lon", "tm", None),
        P("lon", "tm", None),
        P("lon", "tm", None),
    )
    return jax.shard_map(
        body,
        mesh=mesh,
        in_specs=placed,
        out_specs=(P("lon", "tm", None), P("lon", "tm", None)),
        check_vma=False,
    )
```

profile of v0, /device:TPU:1, one launch (start us, length us, event | category | flops | bytes accessed | tf_op | source)
XLA Modules:
  0.0 528.1 jit_solution(4248541663391989781)
XLA Ops:
  1.4 8.8 %collective-permute-start = (f32[1,24,256]{2,1,0:T(8,128)S(1)}, f32[1,24,256]{2,1,0:T(8,128)S(1)}, u32[]{:S(2)}, u32[]{:S(2)}) collective-permute-start(f32[1,24,256]{2,1,0:T(8,128)S(1)} %get-tuple-element.70), channel_id=1, source_target_pairs={{0,4},{4,8},{8,12},{12,16},{16,20},{20,24},{24,28},{28,32},{32,36}... | collective-permute-start | bytes 73736 | tf_op jit(solution)/shard_map/ppermute | solution.py:16
  10.2 5.5 %collective-permute-start.1 = (f32[1,24,256]{2,1,0:T(8,128)S(1)}, f32[1,24,256]{2,1,0:T(8,128)S(1)}, u32[]{:S(2)}, u32[]{:S(2)}) collective-permute-start(f32[1,24,256]{2,1,0:T(8,128)S(1)} %get-tuple-element.69), channel_id=1, source_target_pairs={{4,0},{8,4},{12,8},{16,12},{20,16},{24,20},{28,24},{32,28},{36,32}... | collective-permute-start | bytes 73736 | tf_op jit(solution)/shard_map/ppermute | solution.py:18
  16.7 2.6 collective-permute-done.1
  21.6 4.8 collective-permute-start.3
  28.9 3.1 collective-permute-start.5
  32.0 10.4 %collective-permute-start.4 = (f32[1,24,256]{2,1,0:T(8,128)S(1)}, f32[1,24,256]{2,1,0:T(8,128)S(1)}, u32[]{:S(2)}, u32[]{:S(2)}) collective-permute-start(f32[1,24,256]{2,1,0:T(8,128)S(1)} %get-tuple-element.68), channel_id=1, source_target_pairs={{4,0},{8,4},{12,8},{16,12},{20,16},{24,20},{28,24},{32,28},{36,32}... | collective-permute-start | bytes 73736 | tf_op jit(solution)/shard_map/ppermute | solution.py:18
  43.2 5.7 %collective-permute-start.6 = (f32[10,1,256]{2,1,0:T(1,128)S(1)}, f32[10,1,256]{2,1,0:T(1,128)S(1)}, u32[]{:S(2)}, u32[]{:S(2)}) collective-permute-start(f32[10,1,256]{2,1,0:T(1,128)S(1)} %get-tuple-element.41), channel_id=1, source_target_pairs={{1,0},{2,1},{3,2},{0,3},{5,4},{6,5},{7,6},{4,7},{9,8},{10,9},{11,1... | collective-permute-start | bytes 30728 | tf_op jit(solution)/shard_map/ppermute | solution.py:18
  51.0 4.2 collective-permute-done.7
  57.3 13.9 %collective-permute-start.8 = (f32[1,24,256]{2,1,0:T(8,128)S(1)}, f32[1,24,256]{2,1,0:T(8,128)S(1)}, u32[]{:S(2)}, u32[]{:S(2)}) collective-permute-start(f32[1,24,256]{2,1,0:T(8,128)S(1)} %get-tuple-element.62), channel_id=1, source_target_pairs={{4,0},{8,4},{12,8},{16,12},{20,16},{24,20},{28,24},{32,28},{36,32}... | collective-permute-start | bytes 73736 | tf_op jit(solution)/shard_map/ppermute | solution.py:18
  74.0 3.4 collective-permute-start.11
  77.4 2.8 collective-permute-done.11
  81.1 118.8 %all-reduce.16 = (f32[]{:T(128)}, f32[]{:T(128)}) all-reduce(f32[]{:T(128)} %get-tuple-element.7, f32[]{:T(128)} %get-tuple-element.6), channel_id=1, replica_groups=mesh['lon'=192,'tm'=4] {'lon','tm'}, use_global_device_ids=true, to_apply=%region_1.2 | all-reduce | flops 2 | bytes 16 | tf_op jit(solution)/shard_map/psum | solution.py:106
  201.3 6.7 %collective-permute-start.13 = (f32[1,24,256]{2,1,0:T(8,128)S(1)}, f32[1,24,256]{2,1,0:T(8,128)S(1)}, u32[]{:S(2)}, u32[]{:S(2)}) collective-permute-start(f32[1,24,256]{2,1,0:T(8,128)S(1)} %get-tuple-element.59), channel_id=1, source_target_pairs={{0,4},{4,8},{8,12},{12,16},{16,20},{20,24},{24,28},{28,32},{32,36}... | collective-permute-start | bytes 73736 | tf_op jit(solution)/shard_map/ppermute | solution.py:16
  210.0 7.1 %collective-permute-done.12 = f32[1,24,256]{2,1,0:T(8,128)S(1)} collective-permute-done((f32[1,24,256]{2,1,0:T(8,128)S(1)}, f32[1,24,256]{2,1,0:T(8,128)S(1)}, u32[]{:S(2)}, u32[]{:S(2)}) %collective-permute-start.12) | collective-permute-done | bytes 24608 | tf_op jit(solution)/shard_map/ppermute | solution.py:18
  219.0 3.4 collective-permute-start.15
  222.5 2.7 collective-permute-done.15
  225.4 3.1 collective-permute-start.17
  228.5 2.6 collective-permute-start.16
  231.2 6.4 %collective-permute-done.16 = f32[1,24,256]{2,1,0:T(8,128)S(1)} collective-permute-done((f32[1,24,256]{2,1,0:T(8,128)S(1)}, f32[1,24,256]{2,1,0:T(8,128)S(1)}, u32[]{:S(2)}, u32[]{:S(2)}) %collective-permute-start.16) | collective-permute-done | bytes 24608 | tf_op jit(solution)/shard_map/ppermute | solution.py:18
  239.5 3.4 collective-permute-start.19
  243.0 2.7 collective-permute-done.19
  246.7 113.3 %all-reduce.15 = (f32[]{:T(128)}, f32[]{:T(128)}) all-reduce(f32[]{:T(128)} %get-tuple-element.5, f32[]{:T(128)} %get-tuple-element.4), channel_id=1, replica_groups=mesh['lon'=192,'tm'=4] {'lon','tm'}, use_global_device_ids=true, to_apply=%region_5.6 | all-reduce | flops 2 | bytes 16 | tf_op jit(solution)/shard_map/psum | solution.py:106
  364.7 6.8 %collective-permute-start.21 = (f32[1,24,256]{2,1,0:T(8,128)S(1)}, f32[1,24,256]{2,1,0:T(8,128)S(1)}, u32[]{:S(2)}, u32[]{:S(2)}) collective-permute-start(f32[1,24,256]{2,1,0:T(8,128)S(1)} %get-tuple-element.51), channel_id=1, source_target_pairs={{0,4},{4,8},{8,12},{12,16},{16,20},{20,24},{24,28},{28,32},{32,36}... | collective-permute-start | bytes 73736 | tf_op jit(solution)/shard_map/ppermute | solution.py:16
  373.4 7.1 %collective-permute-done.20 = f32[1,24,256]{2,1,0:T(8,128)S(1)} collective-permute-done((f32[1,24,256]{2,1,0:T(8,128)S(1)}, f32[1,24,256]{2,1,0:T(8,128)S(1)}, u32[]{:S(2)}, u32[]{:S(2)}) %collective-permute-start.20) | collective-permute-done | bytes 24608 | tf_op jit(solution)/shard_map/ppermute | solution.py:18
  382.4 3.4 collective-permute-start.23
  385.9 2.7 collective-permute-done.23
  388.9 3.1 collective-permute-start.25
  392.0 2.6 collective-permute-start.24
  394.6 6.5 %collective-permute-done.24 = f32[1,24,256]{2,1,0:T(8,128)S(1)} collective-permute-done((f32[1,24,256]{2,1,0:T(8,128)S(1)}, f32[1,24,256]{2,1,0:T(8,128)S(1)}, u32[]{:S(2)}, u32[]{:S(2)}) %collective-permute-start.24) | collective-permute-done | bytes 24608 | tf_op jit(solution)/shard_map/ppermute | solution.py:18
  403.0 3.4 collective-permute-start.27
  406.4 2.7 collective-permute-done.27
  410.0 113.2 %all-reduce.14 = (f32[]{:T(128)}, f32[]{:T(128)}) all-reduce(f32[]{:T(128)} %get-tuple-element.3, f32[]{:T(128)} %get-tuple-element.2), channel_id=1, replica_groups=mesh['lon'=192,'tm'=4] {'lon','tm'}, use_global_device_ids=true, to_apply=%region_9.10 | all-reduce | flops 2 | bytes 16 | tf_op jit(solution)/shard_map/psum | solution.py:106
  (69 shorter events, 30.3 us)
Async XLA Ops:
  1.4 14.4 %collective-permute-start = (f32[1,24,256]{2,1,0:T(8,128)S(1)}, f32[1,24,256]{2,1,0:T(8,128)S(1)}, u32[]{:S(2)}, u32[]{:S(2)}) collective-permute-start(f32[1,24,256]{2,1,0:T(8,128)S(1)} %get-tuple-element.70), channel_id=1, source_target_pairs={{0,4},{4,8},{8,12},{12,16},{16,20},{20,24},{24,28},{28,32},{32,36}... | collective-permute-start | bytes 73736 | tf_op jit(solution)/shard_map/ppermute | solution.py:16
  10.2 9.1 %collective-permute-start.1 = (f32[1,24,256]{2,1,0:T(8,128)S(1)}, f32[1,24,256]{2,1,0:T(8,128)S(1)}, u32[]{:S(2)}, u32[]{:S(2)}) collective-permute-start(f32[1,24,256]{2,1,0:T(8,128)S(1)} %get-tuple-element.69), channel_id=1, source_target_pairs={{4,0},{8,4},{12,8},{16,12},{20,16},{24,20},{28,24},{32,28},{36,32}... | collective-permute-start | bytes 73736 | tf_op jit(solution)/shard_map/ppermute | solution.py:18
  19.3 7.1 %collective-permute-start.2 = (f32[10,1,256]{2,1,0:T(1,128)S(1)}, f32[10,1,256]{2,1,0:T(1,128)S(1)}, u32[]{:S(2)}, u32[]{:S(2)}) collective-permute-start(f32[10,1,256]{2,1,0:T(1,128)S(1)} %get-tuple-element.43), channel_id=1, source_target_pairs={{0,1},{1,2},{2,3},{3,0},{4,5},{5,6},{6,7},{7,4},{8,9},{9,10},{10,1... | collective-permute-start | bytes 30728 | tf_op jit(solution)/shard_map/ppermute | solution.py:16
  21.6 5.6 %collective-permute-start.3 = (f32[10,1,256]{2,1,0:T(1,128)S(1)}, f32[10,1,256]{2,1,0:T(1,128)S(1)}, u32[]{:S(2)}, u32[]{:S(2)}) collective-permute-start(f32[10,1,256]{2,1,0:T(1,128)S(1)} %get-tuple-element.44), channel_id=1, source_target_pairs={{1,0},{2,1},{3,2},{0,3},{5,4},{6,5},{7,6},{4,7},{9,8},{10,9},{11,1... | collective-permute-start | bytes 30728 | tf_op jit(solution)/shard_map/ppermute | solution.py:18
  27.3 0.9 copy-start
  27.3 1.0 copy-start.1
  27.3 1.1 copy-start.2
  28.9 13.5 %collective-permute-start.5 = (f32[1,24,256]{2,1,0:T(8,128)S(1)}, f32[1,24,256]{2,1,0:T(8,128)S(1)}, u32[]{:S(2)}, u32[]{:S(2)}) collective-permute-start(f32[1,24,256]{2,1,0:T(8,128)S(1)} %get-tuple-element.67), channel_id=1, source_target_pairs={{0,4},{4,8},{8,12},{12,16},{16,20},{20,24},{24,28},{28,32},{32,36}... | collective-permute-start | bytes 73736 | tf_op jit(solution)/shard_map/ppermute | solution.py:16
  32.0 11.3 %collective-permute-start.4 = (f32[1,24,256]{2,1,0:T(8,128)S(1)}, f32[1,24,256]{2,1,0:T(8,128)S(1)}, u32[]{:S(2)}, u32[]{:S(2)}) collective-permute-start(f32[1,24,256]{2,1,0:T(8,128)S(1)} %get-tuple-element.68), channel_id=1, source_target_pairs={{4,0},{8,4},{12,8},{16,12},{20,16},{24,20},{28,24},{32,28},{36,32}... | collective-permute-start | bytes 73736 | tf_op jit(solution)/shard_map/ppermute | solution.py:18
  43.2 7.8 %collective-permute-start.6 = (f32[10,1,256]{2,1,0:T(1,128)S(1)}, f32[10,1,256]{2,1,0:T(1,128)S(1)}, u32[]{:S(2)}, u32[]{:S(2)}) collective-permute-start(f32[10,1,256]{2,1,0:T(1,128)S(1)} %get-tuple-element.41), channel_id=1, source_target_pairs={{1,0},{2,1},{3,2},{0,3},{5,4},{6,5},{7,6},{4,7},{9,8},{10,9},{11,1... | collective-permute-start | bytes 30728 | tf_op jit(solution)/shard_map/ppermute | solution.py:18
  49.0 6.2 %collective-permute-start.7 = (f32[10,1,256]{2,1,0:T(1,128)S(1)}, f32[10,1,256]{2,1,0:T(1,128)S(1)}, u32[]{:S(2)}, u32[]{:S(2)}) collective-permute-start(f32[10,1,256]{2,1,0:T(1,128)S(1)} %get-tuple-element.42), channel_id=1, source_target_pairs={{0,1},{1,2},{2,3},{3,0},{4,5},{5,6},{6,7},{7,4},{8,9},{9,10},{10,1... | collective-permute-start | bytes 30728 | tf_op jit(solution)/shard_map/ppermute | solution.py:16
  55.4 15.8 %collective-permute-start.9 = (f32[1,24,256]{2,1,0:T(8,128)S(1)}, f32[1,24,256]{2,1,0:T(8,128)S(1)}, u32[]{:S(2)}, u32[]{:S(2)}) collective-permute-start(f32[1,24,256]{2,1,0:T(8,128)S(1)} %get-tuple-element.61), channel_id=1, source_target_pairs={{0,4},{4,8},{8,12},{12,16},{16,20},{20,24},{24,28},{28,32},{32,36}... | collective-permute-start | bytes 73736 | tf_op jit(solution)/shard_map/ppermute | solution.py:16
  57.3 14.7 %collective-permute-start.8 = (f32[1,24,256]{2,1,0:T(8,128)S(1)}, f32[1,24,256]{2,1,0:T(8,128)S(1)}, u32[]{:S(2)}, u32[]{:S(2)}) collective-permute-start(f32[1,24,256]{2,1,0:T(8,128)S(1)} %get-tuple-element.62), channel_id=1, source_target_pairs={{4,0},{8,4},{12,8},{16,12},{20,16},{24,20},{28,24},{32,28},{36,32}... | collective-permute-start | bytes 73736 | tf_op jit(solution)/shard_map/ppermute | solution.py:18
  72.0 5.4 %collective-permute-start.10 = (f32[10,1,256]{2,1,0:T(1,128)S(1)}, f32[10,1,256]{2,1,0:T(1,128)S(1)}, u32[]{:S(2)}, u32[]{:S(2)}) collective-permute-start(f32[10,1,256]{2,1,0:T(1,128)S(1)} %get-tuple-element.39), channel_id=1, source_target_pairs={{1,0},{2,1},{3,2},{0,3},{5,4},{6,5},{7,6},{4,7},{9,8},{10,9},{11,1... | collective-permute-start | bytes 30728 | tf_op jit(solution)/shard_map/ppermute | solution.py:18
  74.0 6.3 %collective-permute-start.11 = (f32[10,1,256]{2,1,0:T(1,128)S(1)}, f32[10,1,256]{2,1,0:T(1,128)S(1)}, u32[]{:S(2)}, u32[]{:S(2)}) collective-permute-start(f32[10,1,256]{2,1,0:T(1,128)S(1)} %get-tuple-element.40), channel_id=1, source_target_pairs={{0,1},{1,2},{2,3},{3,0},{4,5},{5,6},{6,7},{7,4},{8,9},{9,10},{10,1... | collective-permute-start | bytes 30728 | tf_op jit(solution)/shard_map/ppermute | solution.py:16
  201.3 8.7 %collective-permute-start.13 = (f32[1,24,256]{2,1,0:T(8,128)S(1)}, f32[1,24,256]{2,1,0:T(8,128)S(1)}, u32[]{:S(2)}, u32[]{:S(2)}) collective-permute-start(f32[1,24,256]{2,1,0:T(8,128)S(1)} %get-tuple-element.59), channel_id=1, source_target_pairs={{0,4},{4,8},{8,12},{12,16},{16,20},{20,24},{24,28},{28,32},{32,36}... | collective-permute-start | bytes 73736 | tf_op jit(solution)/shard_map/ppermute | solution.py:16
  208.0 9.1 %collective-permute-start.12 = (f32[1,24,256]{2,1,0:T(8,128)S(1)}, f32[1,24,256]{2,1,0:T(8,128)S(1)}, u32[]{:S(2)}, u32[]{:S(2)}) collective-permute-start(f32[1,24,256]{2,1,0:T(8,128)S(1)} %get-tuple-element.60), channel_id=1, source_target_pairs={{4,0},{8,4},{12,8},{16,12},{20,16},{24,20},{28,24},{32,28},{36,32}... | collective-permute-start | bytes 73736 | tf_op jit(solution)/shard_map/ppermute | solution.py:18
  217.1 5.4 %collective-permute-start.14 = (f32[10,1,256]{2,1,0:T(1,128)S(1)}, f32[10,1,256]{2,1,0:T(1,128)S(1)}, u32[]{:S(2)}, u32[]{:S(2)}) collective-permute-start(f32[10,1,256]{2,1,0:T(1,128)S(1)} %get-tuple-element.37), channel_id=1, source_target_pairs={{1,0},{2,1},{3,2},{0,3},{5,4},{6,5},{7,6},{4,7},{9,8},{10,9},{11,1... | collective-permute-start | bytes 30728 | tf_op jit(solution)/shard_map/ppermute | solution.py:18
  219.0 6.2 %collective-permute-start.15 = (f32[10,1,256]{2,1,0:T(1,128)S(1)}, f32[10,1,256]{2,1,0:T(1,128)S(1)}, u32[]{:S(2)}, u32[]{:S(2)}) collective-permute-start(f32[10,1,256]{2,1,0:T(1,128)S(1)} %get-tuple-element.38), channel_id=1, source_target_pairs={{0,1},{1,2},{2,3},{3,0},{4,5},{5,6},{6,7},{7,4},{8,9},{9,10},{10,1... | collective-permute-start | bytes 30728 | tf_op jit(solution)/shard_map/ppermute | solution.py:16
  225.4 5.7 %collective-permute-start.17 = (f32[1,24,256]{2,1,0:T(8,128)S(1)}, f32[1,24,256]{2,1,0:T(8,128)S(1)}, u32[]{:S(2)}, u32[]{:S(2)}) collective-permute-start(f32[1,24,256]{2,1,0:T(8,128)S(1)} %get-tuple-element.53), channel_id=1, source_target_pairs={{0,4},{4,8},{8,12},{12,16},{16,20},{20,24},{24,28},{28,32},{32,36}... | collective-permute-start | bytes 73736 | tf_op jit(solution)/shard_map/ppermute | solution.py:16
  228.5 9.1 %collective-permute-start.16 = (f32[1,24,256]{2,1,0:T(8,128)S(1)}, f32[1,24,256]{2,1,0:T(8,128)S(1)}, u32[]{:S(2)}, u32[]{:S(2)}) collective-permute-start(f32[1,24,256]{2,1,0:T(8,128)S(1)} %get-tuple-element.54), channel_id=1, source_target_pairs={{4,0},{8,4},{12,8},{16,12},{20,16},{24,20},{28,24},{32,28},{36,32}... | collective-permute-start | bytes 73736 | tf_op jit(solution)/shard_map/ppermute | solution.py:18
  237.6 5.4 %collective-permute-start.18 = (f32[10,1,256]{2,1,0:T(1,128)S(1)}, f32[10,1,256]{2,1,0:T(1,128)S(1)}, u32[]{:S(2)}, u32[]{:S(2)}) collective-permute-start(f32[10,1,256]{2,1,0:T(1,128)S(1)} %get-tuple-element.35), channel_id=1, source_target_pairs={{1,0},{2,1},{3,2},{0,3},{5,4},{6,5},{7,6},{4,7},{9,8},{10,9},{11,1... | collective-permute-start | bytes 30728 | tf_op jit(solution)/shard_map/ppermute | solution.py:18
  239.5 6.2 %collective-permute-start.19 = (f32[10,1,256]{2,1,0:T(1,128)S(1)}, f32[10,1,256]{2,1,0:T(1,128)S(1)}, u32[]{:S(2)}, u32[]{:S(2)}) collective-permute-start(f32[10,1,256]{2,1,0:T(1,128)S(1)} %get-tuple-element.36), channel_id=1, source_target_pairs={{0,1},{1,2},{2,3},{3,0},{4,5},{5,6},{6,7},{7,4},{8,9},{9,10},{10,1... | collective-permute-start | bytes 30728 | tf_op jit(solution)/shard_map/ppermute | solution.py:16
  364.7 8.7 %collective-permute-start.21 = (f32[1,24,256]{2,1,0:T(8,128)S(1)}, f32[1,24,256]{2,1,0:T(8,128)S(1)}, u32[]{:S(2)}, u32[]{:S(2)}) collective-permute-start(f32[1,24,256]{2,1,0:T(8,128)S(1)} %get-tuple-element.51), channel_id=1, source_target_pairs={{0,4},{4,8},{8,12},{12,16},{16,20},{20,24},{24,28},{28,32},{32,36}... | collective-permute-start | bytes 73736 | tf_op jit(solution)/shard_map/ppermute | solution.py:16
  371.4 9.1 %collective-permute-start.20 = (f32[1,24,256]{2,1,0:T(8,128)S(1)}, f32[1,24,256]{2,1,0:T(8,128)S(1)}, u32[]{:S(2)}, u32[]{:S(2)}) collective-permute-start(f32[1,24,256]{2,1,0:T(8,128)S(1)} %get-tuple-element.52), channel_id=1, source_target_pairs={{4,0},{8,4},{12,8},{16,12},{20,16},{24,20},{28,24},{32,28},{36,32}... | collective-permute-start | bytes 73736 | tf_op jit(solution)/shard_map/ppermute | solution.py:18
  380.5 5.4 %collective-permute-start.22 = (f32[10,1,256]{2,1,0:T(1,128)S(1)}, f32[10,1,256]{2,1,0:T(1,128)S(1)}, u32[]{:S(2)}, u32[]{:S(2)}) collective-permute-start(f32[10,1,256]{2,1,0:T(1,128)S(1)} %get-tuple-element.33), channel_id=1, source_target_pairs={{1,0},{2,1},{3,2},{0,3},{5,4},{6,5},{7,6},{4,7},{9,8},{10,9},{11,1... | collective-permute-start | bytes 30728 | tf_op jit(solution)/shard_map/ppermute | solution.py:18
  382.4 6.2 %collective-permute-start.23 = (f32[10,1,256]{2,1,0:T(1,128)S(1)}, f32[10,1,256]{2,1,0:T(1,128)S(1)}, u32[]{:S(2)}, u32[]{:S(2)}) collective-permute-start(f32[10,1,256]{2,1,0:T(1,128)S(1)} %get-tuple-element.34), channel_id=1, source_target_pairs={{0,1},{1,2},{2,3},{3,0},{4,5},{5,6},{6,7},{7,4},{8,9},{9,10},{10,1... | collective-permute-start | bytes 30728 | tf_op jit(solution)/shard_map/ppermute | solution.py:16
  388.9 5.7 %collective-permute-start.25 = (f32[1,24,256]{2,1,0:T(8,128)S(1)}, f32[1,24,256]{2,1,0:T(8,128)S(1)}, u32[]{:S(2)}, u32[]{:S(2)}) collective-permute-start(f32[1,24,256]{2,1,0:T(8,128)S(1)} %get-tuple-element.45), channel_id=1, source_target_pairs={{0,4},{4,8},{8,12},{12,16},{16,20},{20,24},{24,28},{28,32},{32,36}... | collective-permute-start | bytes 73736 | tf_op jit(solution)/shard_map/ppermute | solution.py:16
  392.0 9.1 %collective-permute-start.24 = (f32[1,24,256]{2,1,0:T(8,128)S(1)}, f32[1,24,256]{2,1,0:T(8,128)S(1)}, u32[]{:S(2)}, u32[]{:S(2)}) collective-permute-start(f32[1,24,256]{2,1,0:T(8,128)S(1)} %get-tuple-element.46), channel_id=1, source_target_pairs={{4,0},{8,4},{12,8},{16,12},{20,16},{24,20},{28,24},{32,28},{36,32}... | collective-permute-start | bytes 73736 | tf_op jit(solution)/shard_map/ppermute | solution.py:18
  401.0 5.4 %collective-permute-start.26 = (f32[10,1,256]{2,1,0:T(1,128)S(1)}, f32[10,1,256]{2,1,0:T(1,128)S(1)}, u32[]{:S(2)}, u32[]{:S(2)}) collective-permute-start(f32[10,1,256]{2,1,0:T(1,128)S(1)} %get-tuple-element.31), channel_id=1, source_target_pairs={{1,0},{2,1},{3,2},{0,3},{5,4},{6,5},{7,6},{4,7},{9,8},{10,9},{11,1... | collective-permute-start | bytes 30728 | tf_op jit(solution)/shard_map/ppermute | solution.py:18
  403.0 6.2 %collective-permute-start.27 = (f32[10,1,256]{2,1,0:T(1,128)S(1)}, f32[10,1,256]{2,1,0:T(1,128)S(1)}, u32[]{:S(2)}, u32[]{:S(2)}) collective-permute-start(f32[10,1,256]{2,1,0:T(1,128)S(1)} %get-tuple-element.32), channel_id=1, source_target_pairs={{0,1},{1,2},{2,3},{3,0},{4,5},{5,6},{6,7},{7,4},{8,9},{9,10},{10,1... | collective-permute-start | bytes 30728 | tf_op jit(solution)/shard_map/ppermute | solution.py:16
where the time goes:
time: 529 us; the launch traced here: 528 us
  blocking collectives  345 us (65%)
  starting transfers between devices  113 us (21%)
  waiting for transfers between devices  49.9 us (9%)
  between operations  11.2 us (2%)
    psum x3, blocking collectives, two_sums(): lax.psum((jnp.sum(residual * scaled), jnp.sum(image * scaled)), ('lon', '...  345 us
    ppermute x14, starting transfers between devices, padded(): lax.ppermute(head, axis, [((i + 1) % count, i) for i in range(count)])  58.9 us
    ppermute x14, starting transfers between devices, padded(): lax.ppermute(tail, axis, [(i, (i + 1) % count) for i in range(count)])  54.5 us
    ppermute x14, waiting for transfers between devices, padded(): lax.ppermute(head, axis, [((i + 1) % count, i) for i in range(count)])  32.1 us
    ppermute x14, waiting for transfers between devices, padded(): lax.ppermute(tail, axis, [(i, (i + 1) % count) for i in range(count)])  17.8 us
  transfers between devices with their start and end apart: 28, of which 14 were waited for; matrix products, arithmetic and copies ran while one was open for 0% of the time, Pallas kernels for 0%

commit v1 on v0

v1 whole, which is shorter than its diff:
```python
import itertools

import jax
import jax.numpy as jnp
from jax import lax
from jax.experimental import pallas as pl
from jax.experimental.pallas import tpu as pltpu
from jax.sharding import PartitionSpec as P

MESH = pl.DeviceIdType.MESH
SIZES = {"x": 4, "z": 12, "h": 2, "c": 2, "l": 4}
STAGES = (("z", "c"), ("x", "h", "l"))
NX, NT, NA = 8, 24, 256
HX, HT = 3, 8
EX, ET = NX + 2 * HX, NT + 2 * HT
T0, T1 = HT, HT + NT


def place():
    lon, tm = lax.axis_index("lon"), lax.axis_index("tm")
    return {"c": lon % 2, "h": (lon // 2) % 2, "z": (lon // 4) % 12, "x": lon // 48, "l": tm}


def peers(axes):
    here, out = place(), []
    for offset in itertools.product(*[range(SIZES[a]) for a in axes]):
        if any(offset):
            at = dict(here)
            for a, o in zip(axes, offset):
                if o:
                    at[a] = lax.rem(at[a] + o, SIZES[a])
            out.append((((at["x"] * 12 + at["z"]) * 2 + at["h"]) * 2 + at["c"], at["l"]))
    return out


def face(here, there):
    total = here + there
    return jnp.where(total > 0, 2.0 * here * there / jnp.where(total > 0, total, 1.0), 0.0)


def roll(v, step, axis):
    return pltpu.roll(v, step % v.shape[axis], axis)


def solve_kernel(b_in, k_in, h_in, o_in, x_out, r_out, b, k, h, o, fx, ft, fl, d, m,
                 y0, y1, y2, u, v, w1, w2, w3, row, slots,
                 in_sem, s1, r1, s2, r2, s3, r3, sa, ra):
    lon, tm = lax.axis_index("lon"), lax.axis_index("tm")
    east, west = lax.rem(lon + 1, 192), lax.rem(lon + 191, 192)
    up, down = lax.rem(tm + 1, 4), lax.rem(tm + 3, 4)
    stage_peers = [peers(axes) for axes in STAGES]

    barrier = pltpu.get_barrier_semaphore()
    everyone = [(a, t) for a in (east, west) for t in (tm, up, down)] + [(lon, up), (lon, down)]
    for group in stage_peers:
        everyone += group
    for who in everyone:
        pl.semaphore_signal(barrier, inc=1, device_id=who, device_id_type=MESH)

    mine = [
        pltpu.make_async_copy(src, dst.at[pl.ds(HX, NX), pl.ds(T0, NT)], in_sem.at[i])
        for i, (src, dst) in enumerate(((b_in, b), (k_in, k), (h_in, h), (o_in, o)))
    ]
    for copy in mine:
        copy.start()

    @pl.when(tm == 0)
    def _():
        for ref, value in ((h, 0.0), (k, 1.0), (o, 1.0), (b, 0.0), (y1, 0.0), (v, 0.0)):
            ref[:, :T0] = jnp.full((EX, HT, NA), value, jnp.float32)

    @pl.when(tm == 3)
    def _():
        for ref, value in ((h, 0.0), (k, 1.0), (o, 1.0), (b, 0.0), (y1, 0.0), (v, 0.0)):
            ref[:, T1:] = jnp.full((EX, HT, NA), value, jnp.float32)

    pl.semaphore_wait(barrier, len(everyone))

    def exchange(src, off_x, off_t, dst, width, corner, ssem, rsem, base):
        plain, upward, downward = [], [], []
        count = itertools.count(base)

        def make(group, sx, st, nx, nt, dx, dt, who):
            n = next(count)
            group.append(pltpu.make_async_remote_copy(
                src.at[pl.ds(off_x + sx, nx), pl.ds(off_t + st, nt)],
                dst.at[pl.ds(dx, nx), pl.ds(dt, nt)],
                ssem.at[n], rsem.at[n], device_id=who, device_id_type=MESH))

        make(plain, NX - width, 0, width, NT, HX - width, T0, (east, tm))
        make(plain, 0, 0, width, NT, HX + NX, T0, (west, tm))
        make(upward, 0, NT - width, NX, width, HX, T0 - width, (lon, up))
        make(downward, 0, 0, NX, width, HX, T1, (lon, down))
        if corner:
            make(upward, NX - corner, NT - corner, corner, corner, HX - corner, T0 - corner, (east, up))
            make(upward, 0, NT - corner, corner, corner, HX + NX, T0 - corner, (west, up))
            make(downward, NX - corner, 0, corner, corner, HX - corner, T1, (east, down))
            make(downward, 0, 0, corner, corner, HX + NX, T1, (west, down))
        return plain, upward, downward, next(count)

    def start(groups):
        plain, upward, downward = groups[:3]
        for copy in plain:
            copy.start()

        @pl.when(tm < 3)
        def _():
            for copy in upward:
                copy.start()

        @pl.when(tm > 0)
        def _():
            for copy in downward:
                copy.start()

    def received(groups):
        plain, upward, downward = groups[:3]
        for copy in plain:
            copy.wait_recv()

        @pl.when(tm > 0)
        def _():
            for copy in upward:
                copy.wait_recv()

        @pl.when(tm < 3)
        def _():
            for copy in downward:
                copy.wait_recv()

    def sent(groups):
        plain, upward, downward = groups[:3]
        for copy in plain:
            copy.wait_send()

        @pl.when(tm < 3)
        def _():
            for copy in upward:
                copy.wait_send()

        @pl.when(tm > 0)
        def _():
            for copy in downward:
                copy.wait_send()

    first, base = [], 0
    for src, dst, width, corner in ((h_in, h, 3, 2), (k_in, k, 2, 1), (o_in, o, 2, 1), (b_in, b, 2, 1)):
        groups = exchange(src, 0, 0, dst, width, corner, s1, r1, base)
        base = groups[3]
        first.append(groups)
    for groups in first:
        start(groups)
    for copy in mine:
        copy.wait()
    for groups in first:
        received(groups)

    def stencil(field, s):
        here = field[s]
        ftv, flv = ft[s], fl[s]
        near = fx[s] * field[s + 1] + fx[s - 1] * field[s - 1]
        near += ftv * roll(here, -1, 0) + roll(ftv * here, 1, 0)
        near += flv * roll(here, -1, 1) + roll(flv * here, 1, 1)
        return d[s] * here - near

    lat = lax.broadcasted_iota(jnp.int32, (ET, NA), 1)

    @pl.loop(0, EX - 1)
    def _(s):
        fx[s] = face(h[s], h[s + 1])

    @pl.loop(1, EX - 1)
    def _(s):
        here = h[s]
        ftv = face(here, roll(here, -1, 0))
        flv = jnp.where(lat == NA - 1, 0.0, face(here, roll(here, -1, 1)))
        ft[s], fl[s] = ftv, flv
        sides = (fx[s], fx[s - 1], ftv, roll(ftv, 1, 0), flv, roll(flv, 1, 1))
        total, squares = k[s], o[s]
        for f in sides:
            total += f
            squares += f * f
        d[s] = total
        inverse = 1.0 / (total * total + squares)
        m[s] = inverse
        y0[s] = inverse * b[s]

    @pl.loop(2, EX - 2)
    def _(s):
        u[s] = stencil(y0, s)

    @pl.loop(HX, HX + NX)
    def _(s):
        w = (stencil(u, s) + o[s] * y0[s])[T0:T1]
        w1[s - HX] = w
        y1[s, T0:T1] = m[s, T0:T1] * w

    second = exchange(y1, HX, T0, y1, 3, 2, s2, r2, 0)
    start(second)
    received(second)

    @pl.loop(1, EX - 1)
    def _(s):
        u[s] = stencil(y1, s)

    @pl.loop(2, EX - 2)
    def _(s):
        w = stencil(u, s) + o[s] * y1[s]
        w2[s] = w
        y2[s] = m[s] * w

    zero = jnp.zeros((NT, NA), jnp.float32)

    def moments(s, sums):
        w = stencil(y2, s)[T0:T1]
        v[s, T0:T1] = w
        bb, yy0, yy1, yy2 = b[s, T0:T1], y0[s, T0:T1], y1[s, T0:T1], y2[s, T0:T1]
        ww1, ww2 = w1[s - HX], w2[s, T0:T1]
        terms = (bb * yy0, yy0 * ww1, ww1 * yy1, ww1 * yy2, ww2 * yy2, w * w + o[s, T0:T1] * yy2 * yy2)
        return tuple(a + t for a, t in zip(sums, terms))

    sums = lax.fori_loop(HX, HX + NX, moments, (zero,) * 6)

    third = exchange(v, HX, T0, v, 1, 0, s3, r3, 0)
    start(third)

    lane = lax.broadcasted_iota(jnp.int32, (1, 128), 1)
    packed = jnp.zeros((1, 128), jnp.float32)
    for i, part in enumerate(sums):
        packed = jnp.where(lane == i, jnp.sum(part, keepdims=True), packed)

    all_copies = []
    for stage, group in enumerate(stage_peers):
        row[pl.ds(stage, 1)] = packed
        copies = [
            pltpu.make_async_remote_copy(
                row.at[pl.ds(stage, 1)], slots.at[stage, pl.ds(i, 1)], sa.at[stage, i], ra.at[stage, i],
                device_id=who, device_id_type=MESH)
            for i, who in enumerate(group)
        ]
        for copy in copies:
            copy.start()
        all_copies += copies
        if stage == 0:
            received(third)

            @pl.loop(HX, HX + NX)
            def _(s):
                w3[s - HX] = (stencil(v, s) + o[s] * y2[s])[T0:T1]

        for copy in copies:
            copy.wait_recv()
        packed = packed + jnp.sum(slots[stage, : len(group)], axis=0, keepdims=True)

    mu = [packed[:, i : i + 1] for i in range(6)]

    def form(c, shift):
        total = 0.0
        for i, a in enumerate(c):
            for j, e in enumerate(c):
                total = total + a * e * mu[i + j + shift]
        return total

    a0 = mu[0] / mu[1]
    rho1 = [jnp.ones_like(a0), -a0]
    rz1 = form(rho1, 0)
    beta0 = rz1 / mu[0]
    p1 = [1.0 + beta0, -a0]
    a1 = rz1 / form(p1, 1)
    rho2 = [jnp.ones_like(a0), -a0 - a1 * p1[0], -a1 * p1[1]]
    rz2 = form(rho2, 0)
    beta1 = rz2 / rz1
    p2 = [rho2[0] + beta1 * p1[0], rho2[1] + beta1 * p1[1], rho2[2]]
    a2 = rz2 / form(p2, 1)
    c0 = a0 + a1 * p1[0] + a2 * p2[0]
    c1 = a1 * p1[1] + a2 * p2[1]
    c2 = a2 * p2[2]

    @pl.loop(0, NX)
    def _(s):
        e = s + HX
        x_out[s] = c0 * y0[e, T0:T1] + c1 * y1[e, T0:T1] + c2 * y2[e, T0:T1]
        r_out[s] = b[e, T0:T1] - (c0 * w1[s] + c1 * w2[e, T0:T1] + c2 * w3[s])

    for groups in first:
        sent(groups)
    sent(second)
    sent(third)
    for copy in all_copies:
        copy.wait_send()


def body(right_side, kappa_squared, hdiff, obs_weight):
    wide = pltpu.VMEM((EX, ET, NA), jnp.float32)
    block = pltpu.VMEM((NX, NT, NA), jnp.float32)
    most = max(len(list(itertools.product(*[range(SIZES[a]) for a in axes]))) for axes in STAGES)
    dma = pltpu.SemaphoreType.DMA
    return pl.pallas_call(
        solve_kernel,
        out_shape=(jax.ShapeDtypeStruct((NX, NT, NA), jnp.float32),) * 2,
        in_specs=[pl.BlockSpec(memory_space=pl.ANY)] * 4,
        out_specs=(pl.BlockSpec(memory_space=pltpu.VMEM),) * 2,
        scratch_shapes=[wide] * 14 + [block] + [wide] + [block]
        + [pltpu.VMEM((8, 128), jnp.float32), pltpu.VMEM((len(STAGES), most, 128), jnp.float32)]
        + [dma((4,)), dma((32,)), dma((32,)), dma((8,)), dma((8,)), dma((4,)), dma((4,)),
           dma((len(STAGES), most)), dma((len(STAGES), most))],
        compiler_params=pltpu.CompilerParams(
            collective_id=0, has_side_effects=True, vmem_limit_bytes=40 * 2**20
        ),
    )(right_side, kappa_squared, hdiff, obs_weight)


def solution(mesh):
    placed = P("lon", "tm", None)
    return jax.shard_map(
        body, mesh=mesh, in_specs=(placed,) * 4, out_specs=(placed,) * 2, check_vma=False
    )
```

time: 529 us -> 67.5 us (0.13)
  blocking collectives: 345 us -> 0 us
  starting transfers between devices: 113 us -> 0 us
  Pallas kernels: 0 us -> 61.5 us
  waiting for transfers between devices: 49.9 us -> 0 us
  between operations: 11.2 us -> 0.65 us
    psum x3 -> x0, blocking collectives: 345 us -> none  [two_sums(): lax.psum((jnp.sum(residual * scaled), jnp.sum(image * scaled)), ('lon', '...]
    ppermute x28 -> x0, starting transfers between devices: 113 us -> none  [the longest x14 58.9 us: padded(): lax.ppermute(head, axis, [((i + 1) % count, i) for i in range(count)])]
    pallas_call x0 -> x1, Pallas kernels: none -> 61.5 us  [body(): pl.pallas_call(solve_kernel, out_shape=(jax.ShapeDtypeStruct((NX, NT, NA)...]
    ppermute x28 -> x0, waiting for transfers between devices: 49.9 us -> none  [the longest x14 32.1 us: padded(): lax.ppermute(head, axis, [((i + 1) % count, i) for i in range(count)])]
  transfers between devices with their start and end apart: 28 -> 0, of which waited for: 14 -> 0; matrix products, arithmetic and copies ran while one was open for 0% -> 0% of each run, Pallas kernels for 0% -> 0%
where the time goes in v1:
time: 67.5 us; the launch traced here: 67.2 us
  Pallas kernels  61.5 us (91%)
  local copies, waits for them, and re-layouts  5.05 us (7%)
    pallas_call x1, Pallas kernels, body(): pl.pallas_call(solve_kernel, out_shape=(jax.ShapeDtypeStruct((NX, NT, NA)...  61.5 us
    unnamed x10, local copies, waits for them, and re-layouts  5.05 us

profile of v1, /device:TPU:1, one launch (start us, length us, event | category | flops | bytes accessed | tf_op | source)
XLA Modules:
  0.0 67.2 jit_solution(13486176156327871543)
XLA Ops:
  0.6 0.0 copy-start
  0.6 0.9 %copy-done = f32[8,24,256]{2,1,0:T(8,128)S(1)} copy-done((f32[8,24,256]{2,1,0:T(8,128)S(1)}, f32[8,24,256]{2,1,0:T(8,128)}, u32[]{:S(2)}) %copy-start) | copy-done | bytes 196632
  1.6 0.0 copy-start.1
  1.6 0.9 %copy-done.1 = f32[8,24,256]{2,1,0:T(8,128)S(1)} copy-done((f32[8,24,256]{2,1,0:T(8,128)S(1)}, f32[8,24,256]{2,1,0:T(8,128)}, u32[]{:S(2)}) %copy-start.1) | copy-done | bytes 196632
  2.5 0.0 copy-start.2
  2.5 0.9 %copy-done.2 = f32[8,24,256]{2,1,0:T(8,128)S(1)} copy-done((f32[8,24,256]{2,1,0:T(8,128)S(1)}, f32[8,24,256]{2,1,0:T(8,128)}, u32[]{:S(2)}) %copy-start.2) | copy-done | bytes 196632
  3.4 0.0 copy-start.3
  3.4 0.9 %copy-done.3 = f32[8,24,256]{2,1,0:T(8,128)S(1)} copy-done((f32[8,24,256]{2,1,0:T(8,128)S(1)}, f32[8,24,256]{2,1,0:T(8,128)}, u32[]{:S(2)}) %copy-start.3) | copy-done | bytes 196632
  4.3 61.5 %shard_map.59 = (f32[8,24,256]{2,1,0:T(8,128)S(1)}, f32[8,24,256]{2,1,0:T(8,128)S(1)}) custom-call(f32[8,24,256]{2,1,0:T(8,128)S(1)} %copy-done, f32[8,24,256]{2,1,0:T(8,128)S(1)} %copy-done.1, f32[8,24,256]{2,1,0:T(8,128)S(1)} %copy-done.2, f32[8,24,256]{2,1,0:T(8,128)S(1)} %copy-done.3), custom_call_target="tpu_custom_call" | custom-call | tf_op jit(solution)/shard_map/pallas_call | solution.py:298
  65.9 0.7 %copy.8 = f32[8,24,256]{2,1,0:T(8,128)} copy(f32[8,24,256]{2,1,0:T(8,128)S(1)} %get-tuple-element.4) | data formatting | bytes 393216
  66.6 0.7 %copy.9 = f32[8,24,256]{2,1,0:T(8,128)} copy(f32[8,24,256]{2,1,0:T(8,128)S(1)} %get-tuple-element.5) | data formatting | bytes 393216
Async XLA Ops:
  0.6 0.9 %copy-start = (f32[8,24,256]{2,1,0:T(8,128)S(1)}, f32[8,24,256]{2,1,0:T(8,128)}, u32[]{:S(2)}) copy-start(f32[8,24,256]{2,1,0:T(8,128)} %b_in.1) | copy-start | bytes 589828
  1.6 0.9 %copy-start.1 = (f32[8,24,256]{2,1,0:T(8,128)S(1)}, f32[8,24,256]{2,1,0:T(8,128)}, u32[]{:S(2)}) copy-start(f32[8,24,256]{2,1,0:T(8,128)} %k_in.1) | copy-start | bytes 589828
  2.5 0.9 %copy-start.2 = (f32[8,24,256]{2,1,0:T(8,128)S(1)}, f32[8,24,256]{2,1,0:T(8,128)}, u32[]{:S(2)}) copy-start(f32[8,24,256]{2,1,0:T(8,128)} %h_in.1) | copy-start | bytes 589828
  3.4 0.9 %copy-start.3 = (f32[8,24,256]{2,1,0:T(8,128)S(1)}, f32[8,24,256]{2,1,0:T(8,128)}, u32[]{:S(2)}) copy-start(f32[8,24,256]{2,1,0:T(8,128)} %o_in.1) | copy-start | bytes 589828

commit v2 on v1

v2 whole, which is shorter than its diff:
```python
import itertools

import jax
import jax.numpy as jnp
from jax import lax
from jax.experimental import pallas as pl
from jax.experimental.pallas import tpu as pltpu
from jax.sharding import PartitionSpec as P

MESH = pl.DeviceIdType.MESH
SIZES = {"x": 4, "z": 12, "h": 2, "c": 2, "l": 4}
STAGES = (("z", "c"), ("x", "h", "l"))
NX, NT, NA = 8, 24, 256
HX, HT = 3, 8
EX, ET = NX + 2 * HX, NT + 2 * HT
T0, T1 = HT, HT + NT


def place():
    lon, tm = lax.axis_index("lon"), lax.axis_index("tm")
    return {"c": lon % 2, "h": (lon // 2) % 2, "z": (lon // 4) % 12, "x": lon // 48, "l": tm}


def peers(axes):
    here, out = place(), []
    for offset in itertools.product(*[range(SIZES[a]) for a in axes]):
        if any(offset):
            at = dict(here)
            for a, o in zip(axes, offset):
                if o:
                    at[a] = lax.rem(at[a] + o, SIZES[a])
            out.append((((at["x"] * 12 + at["z"]) * 2 + at["h"]) * 2 + at["c"], at["l"]))
    return out


def face(here, there):
    total = here + there
    return jnp.where(total > 0, 2.0 * here * there / jnp.where(total > 0, total, 1.0), 0.0)


def roll(v, step, axis):
    return pltpu.roll(v, step % v.shape[axis], axis)


def solve_kernel(b_in, k_in, h_in, o_in, x_out, r_out,
                 b, k, h, o, fx, ft, fl, d, m, y0, y1, y2, u, v, w1, w2, w3, row, slots,
                 in_sem, s_tm, r_tm, s_lon, r_lon, s_cor, r_cor, sa, ra):
    lon, tm = lax.axis_index("lon"), lax.axis_index("tm")
    east, west = lax.rem(lon + 1, 192), lax.rem(lon + 191, 192)
    up, down = lax.rem(tm + 1, 4), lax.rem(tm + 3, 4)

    barrier = pltpu.get_barrier_semaphore()
    near = [(east, tm), (west, tm), (lon, up), (lon, down), (east, up), (east, down), (west, up), (west, down)]
    for who in near:
        pl.semaphore_signal(barrier, inc=1, device_id=who, device_id_type=MESH)

    mine = [
        pltpu.make_async_copy(src, dst.at[pl.ds(HX, NX), pl.ds(T0, NT)], in_sem.at[i])
        for i, (src, dst) in enumerate(((b_in, b), (k_in, k), (h_in, h), (o_in, o)))
    ]
    for copy in mine:
        copy.start()

    stage_peers = [peers(axes) for axes in STAGES]
    for group in stage_peers:
        for who in group:
            pl.semaphore_signal(barrier, inc=1, device_id=who, device_id_type=MESH)

    edges = ((h, 0.0), (k, 1.0), (o, 1.0), (b, 0.0), (y1, 0.0), (v, 0.0))

    @pl.when(tm == 0)
    def _():
        for ref, value in edges:
            ref[:, :T0] = jnp.full((EX, HT, NA), value, jnp.float32)

    @pl.when(tm == 3)
    def _():
        for ref, value in edges:
            ref[:, T1:] = jnp.full((EX, HT, NA), value, jnp.float32)

    pl.semaphore_wait(barrier, len(near) + sum(map(len, stage_peers)))

    def remote(src, dst, ssem, rsem, who):
        return pltpu.make_async_remote_copy(src, dst, ssem, rsem, device_id=who, device_id_type=MESH)

    class Lon:
        def __init__(self, n, src, off_x, off_t, dst, depth, width=1):
            def part(at):
                return src.at[pl.ds(off_x + at, width), pl.ds(off_t, NT)]

            def halo(at):
                return dst.at[pl.ds(at, width), pl.ds(T0, NT)]

            self.copies = [
                remote(part(NX - depth - width + 1), halo(HX - depth - width + 1),
                       s_lon.at[n, 0], r_lon.at[n, 0], (east, tm)),
                remote(part(depth - 1), halo(HX + NX + depth - 1),
                       s_lon.at[n, 1], r_lon.at[n, 1], (west, tm)),
            ]

        def start(self):
            for copy in self.copies:
                copy.start()

        def received(self):
            for copy in self.copies:
                copy.wait_recv()

        def sent(self):
            for copy in self.copies:
                copy.wait_send()

    class Tm:
        def __init__(self, upward, downward):
            self.upward, self.downward = upward, downward

        def run(self, what, towards, back):
            @pl.when(towards)
            def _():
                for copy in self.upward:
                    getattr(copy, what)()

            @pl.when(back)
            def _():
                for copy in self.downward:
                    getattr(copy, what)()

        def start(self):
            self.run("start", tm < 3, tm > 0)

        def received(self):
            self.run("wait_recv", tm > 0, tm < 3)

        def sent(self):
            self.run("wait_send", tm < 3, tm > 0)

    def rows(n, src, off_x, off_t, dst, width):
        return Tm(
            [remote(src.at[pl.ds(off_x, NX), pl.ds(off_t + NT - width, width)],
                    dst.at[pl.ds(HX, NX), pl.ds(T0 - width, width)], s_tm.at[n, 0], r_tm.at[n, 0], (lon, up))],
            [remote(src.at[pl.ds(off_x, NX), pl.ds(off_t, width)],
                    dst.at[pl.ds(HX, NX), pl.ds(T1, width)], s_tm.at[n, 1], r_tm.at[n, 1], (lon, down))],
        )

    def corners(n, src, off_x, off_t, dst, width):
        def make(i, sx, st, dx, dt, who):
            return remote(src.at[pl.ds(off_x + sx, width), pl.ds(off_t + st, width)],
                          dst.at[pl.ds(dx, width), pl.ds(dt, width)], s_cor.at[n, i], r_cor.at[n, i], who)

        return Tm(
            [make(0, NX - width, NT - width, HX - width, T0 - width, (east, up)),
             make(1, 0, NT - width, HX + NX, T0 - width, (west, up))],
            [make(2, NX - width, 0, HX - width, T1, (east, down)),
             make(3, 0, 0, HX + NX, T1, (west, down))],
        )

    inputs = ((h_in, h), (k_in, k), (o_in, o), (b_in, b))
    tm_first = [rows(i, src, 0, 0, dst, 3 if i == 0 else 2) for i, (src, dst) in enumerate(inputs)]
    lon_first = [Lon(i, src, 0, 0, dst, 1, 2 if i == 0 else 1) for i, (src, dst) in enumerate(inputs)]
    cor_first = [corners(i, src, 0, 0, dst, 2 if i == 0 else 1) for i, (src, dst) in enumerate(inputs)]
    lon_y0 = Lon(4, y0, HX, T0, y0, 2)
    lon_late = [Lon(5, h_in, 0, 0, h, 3), Lon(6, k_in, 0, 0, k, 2)]

    tm_first[0].start()
    lon_first[0].start()
    for i in (1, 2, 3):
        tm_first[i].start()
    for i in (1, 2, 3):
        lon_first[i].start()
    for copies in cor_first:
        copies.start()

    lat = lax.broadcasted_iota(jnp.int32, (ET, NA), 1)

    def stencil(field, s):
        here = field[s]
        ftv, flv = ft[s], fl[s]
        sides = fx[s] * field[s + 1] + fx[s - 1] * field[s - 1]
        sides += ftv * roll(here, -1, 0) + roll(ftv * here, 1, 0)
        sides += flv * roll(here, -1, 1) + roll(flv * here, 1, 1)
        return d[s] * here - sides

    def across(*slabs):
        for s in slabs:
            fx[s] = face(h[s], h[s + 1])

    def within(*slabs):
        for s in slabs:
            here = h[s]
            ft[s] = face(here, roll(here, -1, 0))
            fl[s] = jnp.where(lat == NA - 1, 0.0, face(here, roll(here, -1, 1)))

    def diagonal(*slabs, full=True):
        for s in slabs:
            ftv, flv = ft[s], fl[s]
            around = (fx[s], fx[s - 1], ftv, roll(ftv, 1, 0), flv, roll(flv, 1, 1))
            total = k[s]
            for f in around:
                total += f
            d[s] = total
            if full:
                squares = o[s]
                for f in around:
                    squares += f * f
                inverse = 1.0 / (total * total + squares)
                m[s] = inverse
                y0[s] = inverse * b[s]

    def apply(src, *slabs):
        for s in slabs:
            u[s] = stencil(src, s)

    def next_first(*slabs):
        for s in slabs:
            w = (stencil(u, s) + o[s] * y0[s])[T0:T1]
            w1[s - HX] = w
            y1[s, T0:T1] = m[s, T0:T1] * w

    def next_second(*slabs):
        for s in slabs:
            w = stencil(u, s) + o[s] * y1[s]
            w2[s] = w
            y2[s] = m[s] * w

    for copy in mine:
        copy.wait()
    for copies in tm_first:
        copies.received()
    across(3, 4, 8, 9)
    within(4, 9)
    diagonal(4, 9)
    lon_y0.start()
    for copies in lon_late:
        copies.start()
    across(5, 6, 7)
    within(3, 5, 6, 7, 8, 10)
    diagonal(5, 6, 7, 8)
    apply(y0, 5, 6, 7, 8)
    next_first(6, 7)

    lon_first[0].received()
    cor_first[0].received()
    across(1, 2, 10, 11)
    within(2, 11)
    diagonal(3, 10)
    apply(y0, 4, 9)
    next_first(5, 8)
    for i in (1, 2, 3):
        lon_first[i].received()
        cor_first[i].received()
    diagonal(2, 11)
    apply(y0, 3, 10)
    next_first(4, 9)
    lon_y0.received()
    apply(y0, 2, 11)
    next_first(3, 10)

    lon_y1 = Lon(7, y1, HX, T0, y1, 1, 3)
    tm_y1 = rows(4, y1, HX, T0, y1, 3)
    cor_y1 = corners(4, y1, HX, T0, y1, 2)
    lon_y1.start()
    tm_y1.start()
    cor_y1.start()

    for copies in lon_late:
        copies.received()
    across(0, 12)
    within(1, 12)
    diagonal(1, 12, full=False)
    tm_y1.received()
    apply(y1, 4, 5, 6, 7, 8, 9)
    next_second(5, 6, 7, 8)

    sums = [jnp.zeros((NT, NA), jnp.float32)] * 6

    def moments(*slabs):
        for s in slabs:
            t = stencil(y2, s)[T0:T1]
            v[s, T0:T1] = t
            yy0, yy1, yy2 = y0[s, T0:T1], y1[s, T0:T1], y2[s, T0:T1]
            ww1, ww2 = w1[s - HX], w2[s, T0:T1]
            terms = (b[s, T0:T1] * yy0, yy0 * ww1, ww1 * yy1, ww1 * yy2, ww2 * yy2,
                     t * t + o[s, T0:T1] * yy2 * yy2)
            for i, term in enumerate(terms):
                sums[i] = sums[i] + term

    moments(6, 7)
    lon_y1.received()
    cor_y1.received()
    apply(y1, 1, 2, 3, 10, 11, 12)
    next_second(2, 3, 4, 9, 10, 11)
    moments(3, 4, 5, 8, 9, 10)

    lane = lax.broadcasted_iota(jnp.int32, (1, 128), 1)
    packed = jnp.zeros((1, 128), jnp.float32)
    for i, part in enumerate(sums):
        packed = jnp.where(lane == i, jnp.sum(part, keepdims=True), packed)

    lon_u2 = Lon(8, v, HX, T0, v, 1)
    tm_u2 = rows(5, v, HX, T0, v, 1)
    all_copies = []
    for stage, group in enumerate(stage_peers):
        row[pl.ds(stage, 1)] = packed
        copies = [
            remote(row.at[pl.ds(stage, 1)], slots.at[stage, pl.ds(i, 1)], sa.at[stage, i], ra.at[stage, i], who)
            for i, who in enumerate(group)
        ]
        for copy in copies:
            copy.start()
        all_copies += copies
        if stage == 0:
            lon_u2.start()
            tm_u2.start()
        if stage == 1:
            tm_u2.received()
            lon_u2.received()
            for s in range(HX, HX + NX):
                w3[s - HX] = (stencil(v, s) + o[s] * y2[s])[T0:T1]
        for copy in copies:
            copy.wait_recv()
        packed = packed + jnp.sum(slots[stage, : len(group)], axis=0, keepdims=True)

    mu = [packed[:, i : i + 1] for i in range(6)]

    def form(c, shift):
        total = 0.0
        for i, a in enumerate(c):
            for j, e in enumerate(c):
                total = total + a * e * mu[i + j + shift]
        return total

    a0 = mu[0] / mu[1]
    rho1 = [jnp.ones_like(a0), -a0]
    rz1 = form(rho1, 0)
    beta0 = rz1 / mu[0]
    p1 = [1.0 + beta0, -a0]
    a1 = rz1 / form(p1, 1)
    rho2 = [jnp.ones_like(a0), -a0 - a1 * p1[0], -a1 * p1[1]]
    rz2 = form(rho2, 0)
    beta1 = rz2 / rz1
    p2 = [rho2[0] + beta1 * p1[0], rho2[1] + beta1 * p1[1], rho2[2]]
    a2 = rz2 / form(p2, 1)
    c = (a0 + a1 * p1[0] + a2 * p2[0], a1 * p1[1] + a2 * p2[1], a2 * p2[2])
    c0, c1, c2 = (jnp.broadcast_to(value, (NT, NA)) for value in c)
    for s in range(NX):
        e = s + HX
        x_out[s] = c0 * y0[e, T0:T1] + c1 * y1[e, T0:T1] + c2 * y2[e, T0:T1]
        r_out[s] = b[e, T0:T1] - (c0 * w1[s] + c1 * w2[e, T0:T1] + c2 * w3[s])

    for copies in tm_first + lon_first + cor_first + lon_late + [lon_y0, lon_y1, tm_y1, cor_y1, lon_u2, tm_u2]:
        copies.sent()
    for copy in all_copies:
        copy.wait_send()


def body(right_side, kappa_squared, hdiff, obs_weight):
    wide = pltpu.VMEM((EX, ET, NA), jnp.float32)
    block = pltpu.VMEM((NX, NT, NA), jnp.float32)
    most = max(len(list(itertools.product(*[range(SIZES[a]) for a in axes]))) for axes in STAGES)
    dma = pltpu.SemaphoreType.DMA
    return pl.pallas_call(
        solve_kernel,
        out_shape=(jax.ShapeDtypeStruct((NX, NT, NA), jnp.float32),) * 2,
        in_specs=[pl.BlockSpec(memory_space=pl.ANY)] * 4,
        out_specs=(pl.BlockSpec(memory_space=pltpu.VMEM),) * 2,
        scratch_shapes=[wide] * 14 + [block] + [wide] + [block]
        + [pltpu.VMEM((8, 128), jnp.float32), pltpu.VMEM((len(STAGES), most, 128), jnp.float32)]
        + [dma((4,)), dma((6, 2)), dma((6, 2)), dma((9, 2)), dma((9, 2)), dma((5, 4)), dma((5, 4)),
           dma((len(STAGES), most)), dma((len(STAGES), most))],
        compiler_params=pltpu.CompilerParams(
            collective_id=0, has_side_effects=True, vmem_limit_bytes=62 * 2**20
        ),
    )(right_side, kappa_squared, hdiff, obs_weight)


def solution(mesh):
    placed = P("lon", "tm", None)
    return jax.shard_map(
        body, mesh=mesh, in_specs=(placed,) * 4, out_specs=(placed,) * 2, check_vma=False
    )
```

time: 67.5 us -> 58.3 us (0.86)
  Pallas kernels: 61.5 us -> 55.1 us
  local copies, waits for them, and re-layouts: 5.05 us -> 2.34 us
    pallas_call x1, Pallas kernels: 61.5 us -> 55.1 us  [body(): pl.pallas_call(solve_kernel, out_shape=(jax.ShapeDtypeStruct((NX, NT, NA)...]
    unnamed x10 -> x4, local copies, waits for them, and re-layouts: 5.05 us -> 2.34 us
where the time goes in v2:
time: 58.3 us; the launch traced here: 58.1 us
  Pallas kernels  55.1 us (95%)
  local copies, waits for them, and re-layouts  2.34 us (4%)
  between operations  0.65 us (1%)
    pallas_call x1, Pallas kernels, body(): pl.pallas_call(solve_kernel, out_shape=(jax.ShapeDtypeStruct((NX, NT, NA)...  55.1 us
    unnamed x4, local copies, waits for them, and re-layouts  2.34 us

profile of v2, /device:TPU:1, one launch (start us, length us, event | category | flops | bytes accessed | tf_op | source)
XLA Modules:
  0.0 58.1 jit_solution(4144231020717069753)
XLA Ops:
  0.6 55.1 %shard_map.59 = (f32[8,24,256]{2,1,0:T(8,128)}, f32[8,24,256]{2,1,0:T(8,128)}) custom-call(f32[8,24,256]{2,1,0:T(8,128)} %b_in.1, f32[8,24,256]{2,1,0:T(8,128)} %k_in.1, f32[8,24,256]{2,1,0:T(8,128)} %h_in.1, f32[8,24,256]{2,1,0:T(8,128)} %o_in.1), custom_call_target="tpu_custom_call" | custom-call | tf_op jit(solution)/shard_map/pallas_call | solution.py:361
  55.8 0.0 copy-start
  55.8 1.7 %copy.8 = f32[8,24,256]{2,1,0:T(8,128)} copy(f32[8,24,256]{2,1,0:T(8,128)} %get-tuple-element.4) | data formatting | bytes 393216
  57.5 0.0 copy-done
  57.5 0.7 %copy.9 = f32[8,24,256]{2,1,0:T(8,128)} copy(f32[8,24,256]{2,1,0:T(8,128)S(1)} %copy-done) | data formatting | bytes 393216
Async XLA Ops:
  55.8 1.7 %copy-start = (f32[8,24,256]{2,1,0:T(8,128)S(1)}, f32[8,24,256]{2,1,0:T(8,128)}, u32[]{:S(2)}) copy-start(f32[8,24,256]{2,1,0:T(8,128)} %get-tuple-element.5) | copy-start | bytes 589828

commit v3 on v2

--- a/solution.py
+++ b/solution.py
@@ -9,7 +9,9 @@
 
 MESH = pl.DeviceIdType.MESH
 SIZES = {"x": 4, "z": 12, "h": 2, "c": 2, "l": 4}
-STAGES = (("z", "c"), ("x", "h", "l"))
+PLANES = 2
+REST = 12 - PLANES
+BUDGET = 107 * 2**19
 NX, NT, NA = 8, 24, 256
 HX, HT = 3, 8
 EX, ET = NX + 2 * HX, NT + 2 * HT
@@ -23,13 +25,23 @@
 
 def peers(axes):
     here, out = place(), []
+    lon, tm = lax.axis_index("lon"), lax.axis_index("tm")
+    steps = {"x": 48, "z": 4, "h": 2, "c": 1}
+
+    def moves(axis):
+        at, size, step = here[axis], SIZES[axis], steps.get(axis, 1)
+        return [0] + [step * (i - size * (at + i >= size).astype(jnp.int32)) for i in range(1, size)]
+
+    shifts = {a: moves(a) for a in axes}
     for offset in itertools.product(*[range(SIZES[a]) for a in axes]):
         if any(offset):
-            at = dict(here)
-            for a, o in zip(axes, offset):
-                if o:
-                    at[a] = lax.rem(at[a] + o, SIZES[a])
-            out.append((((at["x"] * 12 + at["z"]) * 2 + at["h"]) * 2 + at["c"], at["l"]))
+            to_lon, to_tm = lon, tm
+            for a, i in zip(axes, offset):
+                if i and a == "l":
+                    to_tm = to_tm + shifts[a][i]
+                elif i:
+                    to_lon = to_lon + shifts[a][i]
+            out.append((to_lon, to_tm))
     return out
 
 
@@ -43,8 +55,9 @@
 
 
 def solve_kernel(b_in, k_in, h_in, o_in, x_out, r_out,
-                 b, k, h, o, fx, ft, fl, d, m, y0, y1, y2, u, v, w1, w2, w3, row, slots,
-                 in_sem, s_tm, r_tm, s_lon, r_lon, s_cor, r_cor, sa, ra):
+                 b, k, h, o, fx, ft, fl, d, m, y0, y1, y2, u, v, w1, w2, w3, early, late, outer, row, gathered, slots, total,
+                 in_sem, s_tm, r_tm, s_lon, r_lon, s_cor, r_cor,
+                 s_gather, r_gather, s_plane, r_plane, s_total, r_total):
     lon, tm = lax.axis_index("lon"), lax.axis_index("tm")
     east, west = lax.rem(lon + 1, 192), lax.rem(lon + 191, 192)
     up, down = lax.rem(tm + 1, 4), lax.rem(tm + 3, 4)
@@ -61,10 +74,26 @@
     for copy in mine:
         copy.start()
 
-    stage_peers = [peers(axes) for axes in STAGES]
-    for group in stage_peers:
-        for who in group:
+    here = place()
+    z, core = here["z"], here["c"]
+    collects = z < PLANES
+    column0 = lon - z * 4 - core
+    plane = peers(("x", "h", "l"))
+
+    def column(at_z, at_core):
+        return (column0 + at_z * 4 + at_core, tm)
+
+    heard_from = jnp.where(z < PLANES + REST // 2, 1, 0)
+    spread = [jnp.where(z == 0, PLANES + REST // 2 + i, PLANES + i) for i in range(REST // 2)]
+
+    @pl.when(collects)
+    def _():
+        for who in plane + peers(("z", "c")):
             pl.semaphore_signal(barrier, inc=1, device_id=who, device_id_type=MESH)
+
+    @pl.when(jnp.logical_not(collects))
+    def _():
+        pl.semaphore_signal(barrier, inc=1, device_id=column(heard_from, core), device_id_type=MESH)
 
     edges = ((h, 0.0), (k, 1.0), (o, 1.0), (b, 0.0), (y1, 0.0), (v, 0.0))
 
@@ -78,7 +107,31 @@
         for ref, value in edges:
             ref[:, T1:] = jnp.full((EX, HT, NA), value, jnp.float32)
 
-    pl.semaphore_wait(barrier, len(near) + sum(map(len, stage_peers)))
+    lat_own = lax.broadcasted_iota(jnp.int32, (NT, NA), 1)
+
+    def own_y0(s):
+        at = h[s, T0:T1]
+        ftv = face(at, roll(at, -1, 0))
+        flv = jnp.where(lat_own == NA - 1, 0.0, face(at, roll(at, -1, 1)))
+        around = (face(at, h[s + 1, T0:T1]), face(h[s - 1, T0:T1], at), ftv, roll(ftv, 1, 0), flv, roll(flv, 1, 1))
+        total, squares = k[s, T0:T1], o[s, T0:T1]
+        for f in around:
+            total += f
+            squares += f * f
+        return b[s, T0:T1] / (total * total + squares)
+
+    for copy in mine:
+        copy.wait()
+    early[0] = own_y0(HX + NX - 2)
+    early[1] = own_y0(HX + 1)
+
+    @pl.when(collects)
+    def _():
+        pl.semaphore_wait(barrier, len(near) + 2 * PLANES - 1 + len(plane) + REST // 2)
+
+    @pl.when(jnp.logical_not(collects))
+    def _():
+        pl.semaphore_wait(barrier, len(near) + 2 * PLANES)
 
     def remote(src, dst, ssem, rsem, who):
         return pltpu.make_async_remote_copy(src, dst, ssem, rsem, device_id=who, device_id_type=MESH)
@@ -158,7 +211,22 @@
     tm_first = [rows(i, src, 0, 0, dst, 3 if i == 0 else 2) for i, (src, dst) in enumerate(inputs)]
     lon_first = [Lon(i, src, 0, 0, dst, 1, 2 if i == 0 else 1) for i, (src, dst) in enumerate(inputs)]
     cor_first = [corners(i, src, 0, 0, dst, 2 if i == 0 else 1) for i, (src, dst) in enumerate(inputs)]
-    lon_y0 = Lon(4, y0, HX, T0, y0, 2)
+    class Pair(Lon):
+        def __init__(self, n, eastward, westward):
+            self.copies = [
+                remote(*eastward, s_lon.at[n, 0], r_lon.at[n, 0], (east, tm)),
+                remote(*westward, s_lon.at[n, 1], r_lon.at[n, 1], (west, tm)),
+            ]
+
+    lon_y0 = Pair(4, (early.at[0], late.at[0]), (early.at[1], late.at[1]))
+    low, high = pl.ds(T0, 1), pl.ds(T1 - 1, 1)
+    inner = (pl.ds(HX + NX - 2, 1), pl.ds(HX + 1, 1))
+    lon_rows = [
+        Pair(9, (y0.at[inner[0], low], outer.at[pl.ds(0, 1), pl.ds(0, 1)]),
+             (y0.at[inner[1], low], outer.at[pl.ds(1, 1), pl.ds(0, 1)])),
+        Pair(10, (y0.at[inner[0], high], outer.at[pl.ds(0, 1), pl.ds(7, 1)]),
+             (y0.at[inner[1], high], outer.at[pl.ds(1, 1), pl.ds(7, 1)])),
+    ]
     lon_late = [Lon(5, h_in, 0, 0, h, 3), Lon(6, k_in, 0, 0, k, 2)]
 
     tm_first[0].start()
@@ -167,6 +235,7 @@
         tm_first[i].start()
     for i in (1, 2, 3):
         lon_first[i].start()
+    lon_y0.start()
     for copies in cor_first:
         copies.start()
 
@@ -222,15 +291,12 @@
             w2[s] = w
             y2[s] = m[s] * w
 
-    for copy in mine:
-        copy.wait()
     for copies in tm_first:
         copies.received()
     across(3, 4, 8, 9)
     within(4, 9)
     diagonal(4, 9)
-    lon_y0.start()
-    for copies in lon_late:
+    for copies in lon_rows + lon_late:
         copies.start()
     across(5, 6, 7)
     within(3, 5, 6, 7, 8, 10)
@@ -251,7 +317,12 @@
     diagonal(2, 11)
     apply(y0, 3, 10)
     next_first(4, 9)
-    lon_y0.received()
+    for copies in [lon_y0] + lon_rows:
+        copies.received()
+    step = lax.broadcasted_iota(jnp.int32, (NT, NA), 0)
+    for side, s in enumerate((1, EX - 2)):
+        layer = jnp.where(step == 0, outer[side, 0:1], late[side])
+        y0[s, T0:T1] = jnp.where(step == NT - 1, outer[side, 7:8], layer)
     apply(y0, 2, 11)
     next_first(3, 10)
 
@@ -298,28 +369,58 @@
 
     lon_u2 = Lon(8, v, HX, T0, v, 1)
     tm_u2 = rows(5, v, HX, T0, v, 1)
-    all_copies = []
-    for stage, group in enumerate(stage_peers):
-        row[pl.ds(stage, 1)] = packed
-        copies = [
-            remote(row.at[pl.ds(stage, 1)], slots.at[stage, pl.ds(i, 1)], sa.at[stage, i], ra.at[stage, i], who)
-            for i, who in enumerate(group)
-        ]
-        for copy in copies:
+    row[pl.ds(0, 1)] = packed
+    targets = [(at_z, at_core) for at_z in range(PLANES) for at_core in range(2)]
+    gather = []
+    for i, (at_z, at_core) in enumerate(targets):
+        back = z - at_z + 12 * (z < at_z).astype(jnp.int32)
+        slot = back * 2 + jnp.where(core == at_core, 0, 1)
+        gather.append((slot != 0, remote(
+            row.at[pl.ds(0, 1)], gathered.at[slot], s_gather.at[i], r_gather.at[slot], column(at_z, at_core))))
+    for other, copy in gather:
+        @pl.when(other)
+        def _():
             copy.start()
-        all_copies += copies
-        if stage == 0:
-            lon_u2.start()
-            tm_u2.start()
-        if stage == 1:
-            tm_u2.received()
-            lon_u2.received()
-            for s in range(HX, HX + NX):
-                w3[s - HX] = (stencil(v, s) + o[s] * y2[s])[T0:T1]
-        for copy in copies:
+
+    lon_u2.start()
+    tm_u2.start()
+
+    exchange = [
+        remote(row.at[pl.ds(1, 1)], slots.at[pl.ds(i, 1)], s_plane.at[i], r_plane.at[i], who)
+        for i, who in enumerate(plane)
+    ]
+    total_out = [
+        remote(total, total, s_total.at[i], r_total.at[0], column(at_z, core)) for i, at_z in enumerate(spread)
+    ]
+
+    @pl.when(collects)
+    def _():
+        value = row[pl.ds(0, 1)]
+        for i in range(1, 24):
+            remote(row.at[pl.ds(0, 1)], gathered.at[i], s_gather.at[0], r_gather.at[i], (east, tm)).wait_recv()
+            value = value + gathered[i]
+        row[pl.ds(1, 1)] = value
+        for copy in exchange:
+            copy.start()
+
+    tm_u2.received()
+    lon_u2.received()
+    for s in range(HX, HX + NX):
+        w3[s - HX] = (stencil(v, s) + o[s] * y2[s])[T0:T1]
+
+    @pl.when(collects)
+    def _():
+        for copy in exchange:
             copy.wait_recv()
-        packed = packed + jnp.sum(slots[stage, : len(group)], axis=0, keepdims=True)
-
+        total[...] = row[pl.ds(1, 1)] + jnp.sum(slots[: len(plane)], axis=0, keepdims=True)
+        for copy in total_out:
+            copy.start()
+
+    @pl.when(jnp.logical_not(collects))
+    def _():
+        total_out[0].wait_recv()
+
+    packed = total[...]
     mu = [packed[:, i : i + 1] for i in range(6)]
 
     def form(c, shift):
@@ -347,16 +448,22 @@
         x_out[s] = c0 * y0[e, T0:T1] + c1 * y1[e, T0:T1] + c2 * y2[e, T0:T1]
         r_out[s] = b[e, T0:T1] - (c0 * w1[s] + c1 * w2[e, T0:T1] + c2 * w3[s])
 
-    for copies in tm_first + lon_first + cor_first + lon_late + [lon_y0, lon_y1, tm_y1, cor_y1, lon_u2, tm_u2]:
+    for copies in tm_first + lon_first + cor_first + lon_late + lon_rows + [lon_y0, lon_y1, tm_y1, cor_y1, lon_u2, tm_u2]:
         copies.sent()
-    for copy in all_copies:
-        copy.wait_send()
+    for other, copy in gather:
+        @pl.when(other)
+        def _():
+            copy.wait_send()
+
+    @pl.when(collects)
+    def _():
+        for copy in exchange + total_out:
+            copy.wait_send()
 
 
 def body(right_side, kappa_squared, hdiff, obs_weight):
     wide = pltpu.VMEM((EX, ET, NA), jnp.float32)
     block = pltpu.VMEM((NX, NT, NA), jnp.float32)
-    most = max(len(list(itertools.product(*[range(SIZES[a]) for a in axes]))) for axes in STAGES)
     dma = pltpu.SemaphoreType.DMA
     return pl.pallas_call(
         solve_kernel,
@@ -364,11 +471,12 @@
         in_specs=[pl.BlockSpec(memory_space=pl.ANY)] * 4,
         out_specs=(pl.BlockSpec(memory_space=pltpu.VMEM),) * 2,
         scratch_shapes=[wide] * 14 + [block] + [wide] + [block]
-        + [pltpu.VMEM((8, 128), jnp.float32), pltpu.VMEM((len(STAGES), most, 128), jnp.float32)]
-        + [dma((4,)), dma((6, 2)), dma((6, 2)), dma((9, 2)), dma((9, 2)), dma((5, 4)), dma((5, 4)),
-           dma((len(STAGES), most)), dma((len(STAGES), most))],
+        + [pltpu.VMEM(shape, jnp.float32) for shape in (
+            (2, NT, NA), (2, NT, NA), (2, 8, NA), (8, 128), (24, 1, 128), (32, 128), (1, 128))]
+        + [dma((4,)), dma((6, 2)), dma((6, 2)), dma((11, 2)), dma((11, 2)), dma((5, 4)), dma((5, 4)),
+           dma((4,)), dma((24,)), dma((32,)), dma((32,)), dma((REST // 2,)), dma((1,))],
         compiler_params=pltpu.CompilerParams(
-            collective_id=0, has_side_effects=True, vmem_limit_bytes=62 * 2**20
+            collective_id=0, has_side_effects=True, vmem_limit_bytes=BUDGET
         ),
     )(right_side, kappa_squared, hdiff, obs_weight)
 

time: 58.3 us -> 53.6 us (0.919)
  Pallas kernels: 55.1 us -> 51.4 us
  local copies, waits for them, and re-layouts: 2.34 us -> 1.36 us
    pallas_call x1, Pallas kernels: 55.1 us -> 51.4 us  [body(): pl.pallas_call(solve_kernel, out_shape=(jax.ShapeDtypeStruct((NX, NT, NA)...]
    unnamed x4 -> x2, local copies, waits for them, and re-layouts: 2.34 us -> 1.36 us
where the time goes in v3:
time: 53.6 us; the launch traced here: 53.4 us
  Pallas kernels  51.4 us (96%)
  local copies, waits for them, and re-layouts  1.36 us (3%)
  between operations  0.64 us (1%)
    pallas_call x1, Pallas kernels, body(): pl.pallas_call(solve_kernel, out_shape=(jax.ShapeDtypeStruct((NX, NT, NA)...  51.4 us
    unnamed x2, local copies, waits for them, and re-layouts  1.36 us

profile of v3, /device:TPU:1, one launch (start us, length us, event | category | flops | bytes accessed | tf_op | source)
XLA Modules:
  0.0 53.4 jit_solution(12183651096097144731)
XLA Ops:
  0.6 51.4 %shard_map.59 = (f32[8,24,256]{2,1,0:T(8,128)S(1)}, f32[8,24,256]{2,1,0:T(8,128)S(1)}) custom-call(f32[8,24,256]{2,1,0:T(8,128)} %b_in.1, f32[8,24,256]{2,1,0:T(8,128)} %k_in.1, f32[8,24,256]{2,1,0:T(8,128)} %h_in.1, f32[8,24,256]{2,1,0:T(8,128)} %o_in.1), custom_call_target="tpu_custom_call" | custom-call | tf_op jit(solution)/shard_map/pallas_call | solution.py:468
  52.1 0.7 %copy.8 = f32[8,24,256]{2,1,0:T(8,128)} copy(f32[8,24,256]{2,1,0:T(8,128)S(1)} %get-tuple-element.4) | data formatting | bytes 393216
  52.7 0.7 %copy.9 = f32[8,24,256]{2,1,0:T(8,128)} copy(f32[8,24,256]{2,1,0:T(8,128)S(1)} %get-tuple-element.5) | data formatting | bytes 393216

commit v4 on v3

--- a/solution.py
+++ b/solution.py
@@ -9,7 +9,7 @@
 
 MESH = pl.DeviceIdType.MESH
 SIZES = {"x": 4, "z": 12, "h": 2, "c": 2, "l": 4}
-PLANES = 2
+PLANES = 3
 REST = 12 - PLANES
 BUDGET = 107 * 2**19
 NX, NT, NA = 8, 24, 256
@@ -83,8 +83,8 @@
     def column(at_z, at_core):
         return (column0 + at_z * 4 + at_core, tm)
 
-    heard_from = jnp.where(z < PLANES + REST // 2, 1, 0)
-    spread = [jnp.where(z == 0, PLANES + REST // 2 + i, PLANES + i) for i in range(REST // 2)]
+    spreads = z == PLANES - 1
+    spread = [PLANES + i for i in range(REST)]
 
     @pl.when(collects)
     def _():
@@ -93,7 +93,7 @@
 
     @pl.when(jnp.logical_not(collects))
     def _():
-        pl.semaphore_signal(barrier, inc=1, device_id=column(heard_from, core), device_id_type=MESH)
+        pl.semaphore_signal(barrier, inc=1, device_id=column(PLANES - 1, core), device_id_type=MESH)
 
     edges = ((h, 0.0), (k, 1.0), (o, 1.0), (b, 0.0), (y1, 0.0), (v, 0.0))
 
@@ -127,7 +127,7 @@
 
     @pl.when(collects)
     def _():
-        pl.semaphore_wait(barrier, len(near) + 2 * PLANES - 1 + len(plane) + REST // 2)
+        pl.semaphore_wait(barrier, len(near) + 2 * PLANES - 1 + len(plane) + jnp.where(spreads, REST, 0))
 
     @pl.when(jnp.logical_not(collects))
     def _():
@@ -413,8 +413,11 @@
         for copy in exchange:
             copy.wait_recv()
         total[...] = row[pl.ds(1, 1)] + jnp.sum(slots[: len(plane)], axis=0, keepdims=True)
-        for copy in total_out:
-            copy.start()
+
+        @pl.when(spreads)
+        def _():
+            for copy in total_out:
+                copy.start()
 
     @pl.when(jnp.logical_not(collects))
     def _():
@@ -457,7 +460,12 @@
 
     @pl.when(collects)
     def _():
-        for copy in exchange + total_out:
+        for copy in exchange:
+            copy.wait_send()
+
+    @pl.when(spreads)
+    def _():
+        for copy in total_out:
             copy.wait_send()
 
 
@@ -474,7 +482,7 @@
         + [pltpu.VMEM(shape, jnp.float32) for shape in (
             (2, NT, NA), (2, NT, NA), (2, 8, NA), (8, 128), (24, 1, 128), (32, 128), (1, 128))]
         + [dma((4,)), dma((6, 2)), dma((6, 2)), dma((11, 2)), dma((11, 2)), dma((5, 4)), dma((5, 4)),
-           dma((4,)), dma((24,)), dma((32,)), dma((32,)), dma((REST // 2,)), dma((1,))],
+           dma((2 * PLANES,)), dma((24,)), dma((32,)), dma((32,)), dma((REST,)), dma((1,))],
         compiler_params=pltpu.CompilerParams(
             collective_id=0, has_side_effects=True, vmem_limit_bytes=BUDGET
         ),

time: 53.6 us -> 53.2 us (level)
  no operation moved by 1% of the time
where the time goes in v4:
time: 53.2 us; the launch traced here: 53.1 us
  Pallas kernels  51.1 us (96%)
  local copies, waits for them, and re-layouts  1.36 us (3%)
  between operations  0.64 us (1%)
    pallas_call x1, Pallas kernels, body(): pl.pallas_call(solve_kernel, out_shape=(jax.ShapeDtypeStruct((NX, NT, NA)...  51.1 us
    unnamed x2, local copies, waits for them, and re-layouts  1.36 us

profile of v4, /device:TPU:1, one launch (start us, length us, event | category | flops | bytes accessed | tf_op | source)
XLA Modules:
  0.0 53.1 jit_solution(12298424030127422649)
XLA Ops:
  0.6 51.1 %shard_map.59 = (f32[8,24,256]{2,1,0:T(8,128)S(1)}, f32[8,24,256]{2,1,0:T(8,128)S(1)}) custom-call(f32[8,24,256]{2,1,0:T(8,128)} %b_in.1, f32[8,24,256]{2,1,0:T(8,128)} %k_in.1, f32[8,24,256]{2,1,0:T(8,128)} %h_in.1, f32[8,24,256]{2,1,0:T(8,128)} %o_in.1), custom_call_target="tpu_custom_call" | custom-call | tf_op jit(solution)/shard_map/pallas_call | solution.py:476
  51.7 0.7 %copy.8 = f32[8,24,256]{2,1,0:T(8,128)} copy(f32[8,24,256]{2,1,0:T(8,128)S(1)} %get-tuple-element.4) | data formatting | bytes 393216
  52.4 0.7 %copy.9 = f32[8,24,256]{2,1,0:T(8,128)} copy(f32[8,24,256]{2,1,0:T(8,128)S(1)} %get-tuple-element.5) | data formatting | bytes 393216

commit v5 on v4

--- a/solution.py
+++ b/solution.py
@@ -55,7 +55,7 @@
 
 
 def solve_kernel(b_in, k_in, h_in, o_in, x_out, r_out,
-                 b, k, h, o, fx, ft, fl, d, m, y0, y1, y2, u, v, w1, w2, w3, early, late, outer, row, gathered, slots, total,
+                 b, k, h, o, fx, ft, fl, d, m, y0, y1, y2, u, v, w1, w2, w3, early, late, edge_k, edge_o, edge_g, outer, row, gathered, slots, total,
                  in_sem, s_tm, r_tm, s_lon, r_lon, s_cor, r_cor,
                  s_gather, r_gather, s_plane, r_plane, s_total, r_total):
     lon, tm = lax.axis_index("lon"), lax.axis_index("tm")
@@ -122,8 +122,11 @@
 
     for copy in mine:
         copy.wait()
-    early[0] = own_y0(HX + NX - 2)
-    early[1] = own_y0(HX + 1)
+    for side, (s, f) in enumerate(((HX + NX - 1, HX + NX - 2), (HX, HX))):
+        inward = face(h[f, T0:T1], h[f + 1, T0:T1])
+        edge_k[side] = k[s, T0:T1] + inward
+        edge_o[side] = o[s, T0:T1] + inward * inward
+        early[side] = inward * own_y0(HX + NX - 2 if side == 0 else HX + 1)
 
     @pl.when(collects)
     def _():
@@ -155,8 +158,8 @@
             for copy in self.copies:
                 copy.start()
 
-        def received(self):
-            for copy in self.copies:
+        def received(self, side=None):
+            for copy in self.copies if side is None else self.copies[side : side + 1]:
                 copy.wait_recv()
 
         def sent(self):
@@ -167,22 +170,24 @@
         def __init__(self, upward, downward):
             self.upward, self.downward = upward, downward
 
-        def run(self, what, towards, back):
+        def run(self, what, towards, back, side=None):
+            part = slice(None) if side is None else slice(side, side + 1)
+
             @pl.when(towards)
             def _():
-                for copy in self.upward:
+                for copy in self.upward[part]:
                     getattr(copy, what)()
 
             @pl.when(back)
             def _():
-                for copy in self.downward:
+                for copy in self.downward[part]:
                     getattr(copy, what)()
 
         def start(self):
             self.run("start", tm < 3, tm > 0)
 
-        def received(self):
-            self.run("wait_recv", tm > 0, tm < 3)
+        def received(self, side=None):
+            self.run("wait_recv", tm > 0, tm < 3, side)
 
         def sent(self):
             self.run("wait_send", tm < 3, tm > 0)
@@ -207,10 +212,16 @@
              make(3, 0, 0, HX + NX, T1, (west, down))],
         )
 
-    inputs = ((h_in, h), (k_in, k), (o_in, o), (b_in, b))
-    tm_first = [rows(i, src, 0, 0, dst, 3 if i == 0 else 2) for i, (src, dst) in enumerate(inputs)]
-    lon_first = [Lon(i, src, 0, 0, dst, 1, 2 if i == 0 else 1) for i, (src, dst) in enumerate(inputs)]
-    cor_first = [corners(i, src, 0, 0, dst, 2 if i == 0 else 1) for i, (src, dst) in enumerate(inputs)]
+    def edge_corners(n, src, dst):
+        def make(i, side, row_at, dx, dt, who):
+            return remote(src.at[pl.ds(side, 1), pl.ds(row_at, 1)], dst.at[pl.ds(dx, 1), pl.ds(dt, 1)],
+                          s_cor.at[n, i], r_cor.at[n, i], who)
+
+        return Tm(
+            [make(0, 0, NT - 1, HX - 1, T0 - 1, (east, up)), make(1, 1, NT - 1, HX + NX, T0 - 1, (west, up))],
+            [make(2, 0, 0, HX - 1, T1, (east, down)), make(3, 1, 0, HX + NX, T1, (west, down))],
+        )
+
     class Pair(Lon):
         def __init__(self, n, eastward, westward):
             self.copies = [
@@ -218,16 +229,24 @@
                 remote(*westward, s_lon.at[n, 1], r_lon.at[n, 1], (west, tm)),
             ]
 
+    def edge_pair(n, src, dst):
+        return Pair(n, (src.at[0], dst.at[HX - 1, pl.ds(T0, NT)]), (src.at[1], dst.at[HX + NX, pl.ds(T0, NT)]))
+
+    inputs = ((h_in, h), (k_in, k), (o_in, o), (b_in, b))
+    tm_first = [rows(i, src, 0, 0, dst, 3 if i == 0 else 2) for i, (src, dst) in enumerate(inputs)]
+    lon_first = [
+        Lon(0, h_in, 0, 0, h, 1), edge_pair(1, edge_k, k), edge_pair(2, edge_o, o), Lon(3, b_in, 0, 0, b, 1),
+    ]
+    cor_first = [
+        corners(0, h_in, 0, 0, h, 2), edge_corners(1, edge_k, k), edge_corners(2, edge_o, o),
+        corners(3, b_in, 0, 0, b, 1),
+    ]
     lon_y0 = Pair(4, (early.at[0], late.at[0]), (early.at[1], late.at[1]))
-    low, high = pl.ds(T0, 1), pl.ds(T1 - 1, 1)
-    inner = (pl.ds(HX + NX - 2, 1), pl.ds(HX + 1, 1))
     lon_rows = [
-        Pair(9, (y0.at[inner[0], low], outer.at[pl.ds(0, 1), pl.ds(0, 1)]),
-             (y0.at[inner[1], low], outer.at[pl.ds(1, 1), pl.ds(0, 1)])),
-        Pair(10, (y0.at[inner[0], high], outer.at[pl.ds(0, 1), pl.ds(7, 1)]),
-             (y0.at[inner[1], high], outer.at[pl.ds(1, 1), pl.ds(7, 1)])),
+        Pair(9 + i, *((edge_g.at[side, pl.ds(at, 1)], outer.at[side, pl.ds(at, 1)]) for side in (0, 1)))
+        for i, at in enumerate((0, 7))
     ]
-    lon_late = [Lon(5, h_in, 0, 0, h, 3), Lon(6, k_in, 0, 0, k, 2)]
+    lon_late = [Lon(5, h_in, 0, 0, h, 2, 2), Lon(6, k_in, 0, 0, k, 2)]
 
     tm_first[0].start()
     lon_first[0].start()
@@ -296,6 +315,9 @@
     across(3, 4, 8, 9)
     within(4, 9)
     diagonal(4, 9)
+    for side, (s, f) in enumerate(((9, 9), (4, 3))):
+        edge_g[side, 0:1] = fx[f, T0 : T0 + 1] * y0[s, T0 : T0 + 1]
+        edge_g[side, 7:8] = fx[f, T1 - 1 : T1] * y0[s, T1 - 1 : T1]
     for copies in lon_rows + lon_late:
         copies.start()
     across(5, 6, 7)
@@ -304,47 +326,12 @@
     apply(y0, 5, 6, 7, 8)
     next_first(6, 7)
 
-    lon_first[0].received()
-    cor_first[0].received()
-    across(1, 2, 10, 11)
-    within(2, 11)
-    diagonal(3, 10)
-    apply(y0, 4, 9)
-    next_first(5, 8)
-    for i in (1, 2, 3):
-        lon_first[i].received()
-        cor_first[i].received()
-    diagonal(2, 11)
-    apply(y0, 3, 10)
-    next_first(4, 9)
-    for copies in [lon_y0] + lon_rows:
-        copies.received()
-    step = lax.broadcasted_iota(jnp.int32, (NT, NA), 0)
-    for side, s in enumerate((1, EX - 2)):
-        layer = jnp.where(step == 0, outer[side, 0:1], late[side])
-        y0[s, T0:T1] = jnp.where(step == NT - 1, outer[side, 7:8], layer)
-    apply(y0, 2, 11)
-    next_first(3, 10)
-
     lon_y1 = Lon(7, y1, HX, T0, y1, 1, 3)
     tm_y1 = rows(4, y1, HX, T0, y1, 3)
     cor_y1 = corners(4, y1, HX, T0, y1, 2)
-    lon_y1.start()
-    tm_y1.start()
-    cor_y1.start()
-
-    for copies in lon_late:
-        copies.received()
-    across(0, 12)
-    within(1, 12)
-    diagonal(1, 12, full=False)
-    tm_y1.received()
-    apply(y1, 4, 5, 6, 7, 8, 9)
-    next_second(5, 6, 7, 8)
-
-    sums = [jnp.zeros((NT, NA), jnp.float32)] * 6
-
-    def moments(*slabs):
+    step = lax.broadcasted_iota(jnp.int32, (NT, NA), 0)
+
+    def moments(sums, *slabs):
         for s in slabs:
             t = stencil(y2, s)[T0:T1]
             v[s, T0:T1] = t
@@ -352,24 +339,84 @@
             ww1, ww2 = w1[s - HX], w2[s, T0:T1]
             terms = (b[s, T0:T1] * yy0, yy0 * ww1, ww1 * yy1, ww1 * yy2, ww2 * yy2,
                      t * t + o[s, T0:T1] * yy2 * yy2)
-            for i, term in enumerate(terms):
-                sums[i] = sums[i] + term
-
-    moments(6, 7)
-    lon_y1.received()
-    cor_y1.received()
-    apply(y1, 1, 2, 3, 10, 11, 12)
-    next_second(2, 3, 4, 9, 10, 11)
-    moments(3, 4, 5, 8, 9, 10)
-
-    lane = lax.broadcasted_iota(jnp.int32, (1, 128), 1)
-    packed = jnp.zeros((1, 128), jnp.float32)
-    for i, part in enumerate(sums):
-        packed = jnp.where(lane == i, jnp.sum(part, keepdims=True), packed)
+            sums = [a + term for a, term in zip(sums, terms)]
+        return sums
+
+    def finish(order):
+        for side in order:
+            def at(i):
+                return EX - 1 - i if side else i
+
+            inward = EX - 2 - 2 if side else 2
+            lon_first[0].received(side)
+            cor_first[0].received(side)
+            across(inward)
+            within(at(2))
+            diagonal(at(3))
+            apply(y0, at(4))
+            next_first(at(5))
+            for i in (1, 2, 3):
+                lon_first[i].received(side)
+                cor_first[i].received(side)
+            edge = at(2)
+            ftv, flv = ft[edge], fl[edge]
+            total, squares = k[edge], o[edge]
+            for f in (fx[inward], ftv, roll(ftv, 1, 0), flv, roll(flv, 1, 1)):
+                total += f
+                squares += f * f
+            d[edge] = total
+            m[edge] = 1.0 / (total * total + squares)
+            here = m[edge] * b[edge]
+            y0[edge] = here
+            apply(y0, at(3))
+            next_first(at(4))
+            for copies in [lon_y0] + lon_rows:
+                copies.received(side)
+            far = jnp.where(step == 0, outer[side, 0:1], late[side])
+            far = jnp.where(step == NT - 1, outer[side, 7:8], far)
+            sides = fx[inward] * y0[at(3)]
+            sides += ftv * roll(here, -1, 0) + roll(ftv * here, 1, 0)
+            sides += flv * roll(here, -1, 1) + roll(flv * here, 1, 1)
+            u[edge, T0:T1] = (total * here - sides)[T0:T1] - far
+            next_first(at(3))
+            lon_y1.copies[1 - side].start()
+        tm_y1.start()
+        cor_y1.start()
+
+        for copies in lon_late:
+            copies.received()
+        across(0, 1, 11, 12)
+        for s, f in ((2, 1), (11, 11)):
+            o[s, T0:T1] = o[s, T0:T1] - fx[f, T0:T1] * fx[f, T0:T1]
+        within(1, 12)
+        diagonal(1, 12, full=False)
+        tm_y1.received()
+        apply(y1, 4, 5, 6, 7, 8, 9)
+        next_second(5, 6, 7, 8)
+        sums = moments([jnp.zeros((NT, NA), jnp.float32)] * 6, 6, 7)
+        for side in order:
+            lon_y1.received(side)
+            cor_y1.received(side)
+            slabs = (12, 11, 10, 9, 8) if side else (1, 2, 3, 4, 5)
+            apply(y1, *slabs[:3])
+            next_second(*slabs[1:4])
+            sums = moments(sums, *slabs[2:])
+        lane = lax.broadcasted_iota(jnp.int32, (1, 128), 1)
+        packed = jnp.zeros((1, 128), jnp.float32)
+        for i, part in enumerate(sums):
+            packed = jnp.where(lane == i, jnp.sum(part, keepdims=True), packed)
+        row[pl.ds(0, 1)] = packed
+
+    @pl.when(core == 1)
+    def _():
+        finish((0, 1))
+
+    @pl.when(core == 0)
+    def _():
+        finish((1, 0))
 
     lon_u2 = Lon(8, v, HX, T0, v, 1)
     tm_u2 = rows(5, v, HX, T0, v, 1)
-    row[pl.ds(0, 1)] = packed
     targets = [(at_z, at_core) for at_z in range(PLANES) for at_core in range(2)]
     gather = []
     for i, (at_z, at_core) in enumerate(targets):
@@ -480,7 +527,7 @@
         out_specs=(pl.BlockSpec(memory_space=pltpu.VMEM),) * 2,
         scratch_shapes=[wide] * 14 + [block] + [wide] + [block]
         + [pltpu.VMEM(shape, jnp.float32) for shape in (
-            (2, NT, NA), (2, NT, NA), (2, 8, NA), (8, 128), (24, 1, 128), (32, 128), (1, 128))]
+            (2, NT, NA), (2, NT, NA), (2, NT, NA), (2, NT, NA), (2, 8, NA), (2, 8, NA), (8, 128), (24, 1, 128), (32, 128), (1, 128))]
         + [dma((4,)), dma((6, 2)), dma((6, 2)), dma((11, 2)), dma((11, 2)), dma((5, 4)), dma((5, 4)),
            dma((2 * PLANES,)), dma((24,)), dma((32,)), dma((32,)), dma((REST,)), dma((1,))],
         compiler_params=pltpu.CompilerParams(

time: 53.2 us -> 53.2 us (level)
  no operation moved by 1% of the time
where the time goes in v5:
time: 53.2 us; the launch traced here: 53.1 us
  Pallas kernels  51.1 us (96%)
  local copies, waits for them, and re-layouts  1.36 us (3%)
  between operations  0.64 us (1%)
    pallas_call x1, Pallas kernels, body(): pl.pallas_call(solve_kernel, out_shape=(jax.ShapeDtypeStruct((NX, NT, NA)...  51.1 us
    unnamed x2, local copies, waits for them, and re-layouts  1.36 us

profile of v5, /device:TPU:1, one launch (start us, length us, event | category | flops | bytes accessed | tf_op | source)
XLA Modules:
  0.0 53.1 jit_solution(3070582373313396430)
XLA Ops:
  0.6 51.1 %shard_map.59 = (f32[8,24,256]{2,1,0:T(8,128)S(1)}, f32[8,24,256]{2,1,0:T(8,128)S(1)}) custom-call(f32[8,24,256]{2,1,0:T(8,128)} %b_in.1, f32[8,24,256]{2,1,0:T(8,128)} %k_in.1, f32[8,24,256]{2,1,0:T(8,128)} %h_in.1, f32[8,24,256]{2,1,0:T(8,128)} %o_in.1), custom_call_target="tpu_custom_call" | custom-call | tf_op jit(solution)/shard_map/pallas_call | solution.py:523
  51.7 0.7 %copy.8 = f32[8,24,256]{2,1,0:T(8,128)} copy(f32[8,24,256]{2,1,0:T(8,128)S(1)} %get-tuple-element.4) | data formatting | bytes 393216
  52.4 0.7 %copy.9 = f32[8,24,256]{2,1,0:T(8,128)} copy(f32[8,24,256]{2,1,0:T(8,128)S(1)} %get-tuple-element.5) | data formatting | bytes 393216
